TPU v7x, 256 devices: a whole 4x4x8 slice. The times are simulated.
256 devices in a mesh: blk: 16 (over x_lo, z), dp: 16 (over x_hi, y, core).
Axes of the slice: x: 4 (x_hi: 2, x_lo: 2; x = x_hi * 2 + x_lo), y: 4, z: 8, core: 2. Of those that a mesh axis runs over, the one named last changes fastest.
Arguments:
- user_emb: bfloat16 [65536, 256], P(('blk', 'dp')), may hold values from -6 to 6
- pos_feat: bfloat16 [65536, 256], P(('blk', 'dp')), may hold values from -6 to 6
- pos_id: int32 [65536], P(('blk', 'dp')), may hold values from 0 to 4095
- neg_feat: bfloat16 [131072, 256], P(('blk', 'dp')), may hold values from -6 to 6
- neg_id: int32 [131072], P(('blk', 'dp')), may hold values from 0 to 4095
- neg_bucket: int32 [131072], P(('blk', 'dp')), may hold values from 0 to 1023
- logq_table: float32 [1024], replicated, may hold values from -4 to 0
- w_in: bfloat16 [256, 2048], replicated, may hold values from -0.375 to 0.375
- w_out: bfloat16 [2048, 256], replicated, may hold values from -0.125 to 0.125
Outputs:
- user_grad: float32 [65536, 256], P(('blk', 'dp'))
- w_in_grad: float32 [256, 2048], replicated
- w_out_grad: float32 [2048, 256], replicated
All inputs are finite; a program needn't handle non-finite values.
Results may differ from a plain program's by a relative error of at most 0.008.
Values may be sent and summed in bfloat16 or wider, within the bound.
No kernel may reach another device: no remote copies, remote signals or barrier semaphores. Data moves between devices by JAX's collectives and lax.ppermute only.
A program may use at most 128 MiB of HBM per device.

v0:
```python
import functools

import jax
import jax.numpy as jnp
from jax import lax
from jax.experimental import pallas as pl
from jax.experimental.pallas import tpu as pltpu
from jax.sharding import Mesh, PartitionSpec as P

AXES = ("x_lo", "z", "x_hi", "y", "core")
SIZES = (2, 8, 2, 4, 2)
BF, F32, I32 = jnp.bfloat16, jnp.float32, jnp.int32
SCALE = 0.125
SMALL = 2.0**-64
E, H, U, N = 256, 2048, 256, 512
NN = 2 * N
ROWS = NN + U
TILE = 256
CHUNKS = H // TILE
NZ = 8
ORDER = (3, 2, 1)
OFFSETS = (0, -1, 1, -2, 2, -3, 3, 4)
FIRST = 7
VMEM_LIMIT = 24 * 1024 * 1024

WIDE = 512
NT = (((1,), (1,)), ((), ()))
TN = (((0,), (0,)), ((), ()))


def params(limit=VMEM_LIMIT):
    return pltpu.CompilerParams(vmem_limit_bytes=limit)


def cost(flops, nbytes, trans=0):
    return pl.CostEstimate(flops=int(flops), bytes_accessed=int(nbytes), transcendentals=int(trans))


def whole(shape):
    return pl.BlockSpec(shape, lambda *_: (0,) * len(shape))


def mm(a, b):
    return jnp.dot(a, b, preferred_element_type=F32)


def start(src, dst, sem):
    copy = pltpu.make_async_copy(src, dst, sem)
    copy.start()
    return copy


def pack_kernel(user_hbm, pid_hbm, feat_hbm, nid_hbm, bucket_hbm, mine_ref, near_ref, pid_ref, nid_ref, bucket_ref, sems):
    copies = [
        start(pid_hbm, pid_ref, sems.at[0]),
        start(nid_hbm, nid_ref, sems.at[1]),
        start(bucket_hbm, bucket_ref, sems.at[2]),
        start(user_hbm, mine_ref.at[0:U], sems.at[3]),
        start(feat_hbm, near_ref.at[0:N], sems.at[4]),
    ]
    row = lax.broadcasted_iota(I32, (16, E), 0)

    def tail(digits):
        out = jnp.zeros((16, E), F32)
        for i, digit in enumerate(digits):
            out = jnp.where(row == i, digit.astype(F32), out)
        return out.astype(BF)

    def digits(ids, bits):
        ids = [ids[:, i : i + 256] for i in range(0, ids.shape[1], 256)]
        return [i >> bits for i in ids] + [i & (2**bits - 1) for i in ids]

    for copy in copies[:3]:
        copy.wait()
    mine_ref[U : U + 16] = tail(digits(pid_ref[...], 6))
    near_ref[N : N + 16] = tail(digits(nid_ref[...], 6) + digits(bucket_ref[...], 5))
    for copy in copies[3:]:
        copy.wait()


def pack(user_emb, pos_id, neg_feat, neg_id, neg_bucket):
    vm = pl.BlockSpec(memory_space=pltpu.VMEM)
    return pl.pallas_call(
        pack_kernel,
        in_specs=[pl.BlockSpec(memory_space=pltpu.HBM)] * 5,
        out_specs=[vm] * 2,
        out_shape=[jax.ShapeDtypeStruct((U + 16, E), BF), jax.ShapeDtypeStruct((N + 16, E), BF)],
        scratch_shapes=[
            pltpu.VMEM((1, U), I32),
            pltpu.VMEM((1, N), I32),
            pltpu.VMEM((1, N), I32),
            pltpu.SemaphoreType.DMA((5,)),
        ],
        compiler_params=params(60 * 1024 * 1024),
        cost_estimate=cost(1e10, 1e6),
        name="pack",
    )(user_emb, pos_id.reshape(1, U), neg_feat, neg_id.reshape(1, N), neg_bucket.reshape(1, N))


def hidden(feat, w_in_ref):
    return jnp.maximum(mm(feat, w_in_ref[...]), 0.0).astype(BF)


def hidden_kernel(near_ref, pos_ref, w_in_ref, hid_ref, feat_ref, w_in_out):
    for m, feat in enumerate((near_ref[0:TILE], near_ref[TILE:N], pos_ref[...])):
        rows = slice(m * TILE, (m + 1) * TILE)
        feat_ref[rows] = feat
        hid_ref[rows] = hidden(feat, w_in_ref)
    w_in_out[...] = w_in_ref[...]


def embed_kernel(hid_ref, w_out_ref, emb_ref, pemb_ref, w_out_out):
    w_out_out[...] = w_out_ref[...]
    for m, (ref, first) in enumerate([(emb_ref, 0), (emb_ref, TILE), (pemb_ref, 0)]):
        hid = hid_ref[m * TILE : (m + 1) * TILE]
        ref[first : first + TILE] = mm(hid, w_out_ref[...]).astype(BF)


def far_kernel(near_ref, far_ref, w_in_ref, w_out_ref, table_ref, hid_ref, emb_ref, nid_ref, bias_ref):
    lane = lax.broadcasted_iota(I32, (TILE, 128), 1).astype(F32)
    for side, tail in enumerate((near_ref[N : N + 16], far_ref[N : N + 16])):
        tail = jnp.concatenate([tail.astype(F32), jnp.zeros((112, E), F32)], axis=0).T
        for block in range(2):
            rows = slice((2 * side + block) * TILE, (2 * side + block + 1) * TILE)
            nid = tail[:, block : block + 1] * 64.0 + tail[:, block + 2 : block + 3]
            nid_ref[rows] = jnp.broadcast_to(nid, (TILE, 128))
            bucket = tail[:, block + 4 : block + 5] * 32.0 + tail[:, block + 6 : block + 7]
            found = jnp.zeros((TILE, 128), F32)
            for b in range(8):
                found = found + jnp.where(bucket == lane + 128.0 * b, table_ref[b : b + 1], 0.0)
            bias_ref[rows] = jnp.broadcast_to(jnp.sum(found, axis=1, keepdims=True), (TILE, 128))
    for m in range(N // TILE):
        rows = slice(m * TILE, (m + 1) * TILE)
        hid = hidden(far_ref[rows], w_in_ref)
        hid_ref[rows] = hid
        emb_ref[rows] = mm(hid, w_out_ref[...]).astype(BF)


def in_vmem(kernel, name, flops, outs, *args, scratch=()):
    vm = pl.BlockSpec(memory_space=pltpu.VMEM)
    return pl.pallas_call(
        kernel,
        in_specs=[vm] * len(args),
        out_specs=[vm] * len(outs),
        out_shape=[jax.ShapeDtypeStruct(shape, dtype) for shape, dtype in outs],
        scratch_shapes=list(scratch),
        compiler_params=params(14 * 1024 * 1024),
        cost_estimate=cost(flops, 4e6),
        name=name,
    )(*args)


def twice(x):
    return jnp.concatenate([x, x], axis=1)


def home(z, k):
    return (z + OFFSETS[k] + NZ) & (NZ - 1)


def score_kernel(ks, near_emb, far_emb, nid_ref, bias_ref, pemb_ref, tloc_in, tin_in, *rest):
    users = rest[: len(ks)]
    tloc_ref, tin_ref, pexp_ref, kept_ref, kf = rest[len(ks) :]
    z = lax.axis_index("z")
    tloc_ref[...] = tloc_in[...]
    tin_ref[...] = tin_in[...]
    if ks[0] == 0:
        prod = users[0][0:U].astype(F32) * pemb_ref[...].astype(F32)
        prod = (prod[:, 0:128] + prod[:, 128:256]).T
        pexp_ref[...] = jnp.exp(SCALE * jnp.sum(prod, axis=0, keepdims=True))
    else:
        pexp_ref[...] = jnp.zeros_like(pexp_ref)
    for i, k in enumerate(ks):
        u = (users[i][0:U].astype(F32) * SCALE).astype(BF)
        tail = users[i][U : U + 16].astype(F32)
        pid = tail[0:1] * 64.0 + tail[1:2]
        total = jnp.zeros((8, U), F32)
        for m in range(NN // TILE):
            rows = slice(m * TILE, (m + 1) * TILE)
            emb = near_emb[rows] if m < 2 else far_emb[(m - 2) * TILE : (m - 1) * TILE]
            sc = lax.dot_general(emb, u, NT, preferred_element_type=F32) - twice(bias_ref[rows])
            kept = jnp.where(twice(nid_ref[rows]) != pid, jnp.exp(sc), 0.0)
            kf[rows] = kept
            total = total + jnp.sum(kept.reshape(TILE // 8, 8, U), axis=0)
        t = jnp.sum(total, axis=0, keepdims=True)
        shrink = jnp.where(t > 1.0, SMALL, 1.0)
        inv = jnp.where(t > 0.0, 1.0 / (t * shrink), 0.0)
        @pl.loop(0, NN // TILE)
        def _(m, i=i, shrink=shrink, inv=inv):
            rows = pl.ds(pl.multiple_of(m * TILE, TILE), TILE)
            kept_ref[rows, i * U : (i + 1) * U] = ((kf[rows, :] * shrink) * inv).astype(BF)

        row = pl.ds(home(z, k), 1)
        tloc_ref[row, :] = t
        tin_ref[row, :] = t + pexp_ref[...] if k == 0 else t


def score(ks, near_emb, far_emb, nid, bias, pemb, tloc, tin, users):
    vm = pl.BlockSpec(memory_space=pltpu.VMEM)
    n = len(ks)
    return pl.pallas_call(
        functools.partial(score_kernel, ks),
        in_specs=[vm] * (7 + n),
        out_specs=[vm] * 4,
        out_shape=[
            jax.ShapeDtypeStruct((NZ, U), F32),
            jax.ShapeDtypeStruct((NZ, U), F32),
            jax.ShapeDtypeStruct((1, U), F32),
            jax.ShapeDtypeStruct((NN, n * U), BF),
        ],
        scratch_shapes=[pltpu.VMEM((NN, U), F32)],
        compiler_params=params(14 * 1024 * 1024),
        cost_estimate=cost(2 * n * U * NN * E, 5e6, n * U * NN),
        name="score",
    )(near_emb, far_emb, nid, bias, pemb, tloc, tin, *[users[k] for k in ks])


def ratios(tot_ref, tloc_ref, pexp_ref, ratio, rel):
    z = lax.axis_index("z")
    tot = tot_ref[...]
    shrink = jnp.where(tot > 1.0, SMALL, 1.0)
    ratio[...] = (tloc_ref[...] * shrink) * (1.0 / (tot * shrink))
    own = tot_ref[pl.ds(z, 1), :]
    shrink = jnp.where(own > 1.0, SMALL, 1.0)
    pprob = (pexp_ref[...] * shrink) * (1.0 / (own * shrink))
    rel[...] = jnp.zeros_like(rel)
    for k in range(NZ):
        rel[k : k + 1] = SCALE * ratio[pl.ds(home(z, k), 1), :]
    rel[NZ : NZ + 1] = SCALE * (pprob - 1.0)
    return rel[...].T


RATIOS = [pltpu.VMEM((NZ, U), F32), pltpu.VMEM((128, U), F32)]


def item_grad_kernel(tot_ref, tloc_ref, pexp_ref, kept_a, kept_b, *rest):
    users = rest[:NZ]
    g_ref, wu, ratio, rel = rest[NZ:]
    cols = ratios(tot_ref, tloc_ref, pexp_ref, ratio, rel)
    for k in range(NZ):
        wu[k * U : (k + 1) * U] = (users[k][0:U].astype(F32) * cols[:, k : k + 1]).astype(BF)
    g_ref[N : N + U] = (users[0][0:U].astype(F32) * cols[:, NZ : NZ + 1]).astype(BF)
    for m in range(NN // TILE):
        rows = slice(m * TILE, (m + 1) * TILE)
        g = mm(kept_a[rows], wu[0 : FIRST * U]) + mm(kept_b[rows], wu[FIRST * U :])
        first = m * TILE if m < 2 else m * TILE + U
        g_ref[first : first + TILE] = g.astype(BF)


def user_grad_kernel(tot_ref, tloc_ref, pexp_ref, kept_a, kept_b, near_emb, far_emb, pemb_ref, *rest):
    keep_ref, send_ref, pterm_ref, ratio, rel = rest
    z = lax.axis_index("z")
    cols = ratios(tot_ref, tloc_ref, pexp_ref, ratio, rel)
    pterm_ref[...] = pemb_ref[...].astype(F32) * cols[:, NZ : NZ + 1]
    for k in range(NZ):
        kept, i = (kept_a, k) if k < FIRST else (kept_b, k - FIRST)
        cols_k = slice(i * U, (i + 1) * U)
        ug = lax.dot_general(kept[0:N, cols_k], near_emb[...], TN, preferred_element_type=F32)
        ug = ug + lax.dot_general(kept[N:NN, cols_k], far_emb[...], TN, preferred_element_type=F32)
        apart = jnp.bitwise_xor(home(z, k), z)
        place = (apart & 2) + (apart >> 2)
        (send_ref if OFFSETS[k] % 2 else keep_ref)[place] = (ug * cols[:, k : k + 1]).astype(BF)


def item_grads(tot, tloc, pexp, kept_a, kept_b, users):
    scratch = [pltpu.VMEM((NZ * U, E), BF)] + RATIOS
    args = (tot, tloc, pexp, kept_a, kept_b, *users)
    return in_vmem(item_grad_kernel, "items", 2 * NZ * U * NN * E, [((ROWS, E), BF)], *args, scratch=scratch)[0]


def user_grads(*args):
    outs = [((NZ // 2, U, E), BF), ((NZ // 2, U, E), BF), ((U, E), F32)]
    return in_vmem(user_grad_kernel, "users", 2 * NZ * U * NN * E, outs, *args, scratch=RATIOS)


def order():
    core = lax.axis_index("core")
    xx, y = near(lax.axis_index("x_hi") * 2 + lax.axis_index("x_lo")), near(lax.axis_index("y"))
    return core, jnp.where(core == 0, xx, y), jnp.where(core == 0, y, xx)


def back_kernel(mine, g_ref, feat_ref, far_ref, w_out_ref, hid_ref, far_hid, out_ref):
    core, first, second = order()
    if not mine:
        core, first, second = 1 - core, second, first
    for c in range(2):
        cols = pl.ds(pl.multiple_of(core * (H // 2) + c * WIDE, WIDE), WIDE)
        w_in = w_out = 0.0
        for rows, feat, hid in ((slice(0, N + U), feat_ref, hid_ref), (slice(N + U, ROWS), far_ref, far_hid)):
            hid = hid[:, cols]
            g = g_ref[rows]
            back = lax.dot_general(g, w_out_ref[cols], NT, preferred_element_type=F32)
            back = jnp.where(hid > 0, back, 0.0).astype(BF)
            w_in += lax.dot_general(feat[0 : g.shape[0]], back, TN, preferred_element_type=F32)
            w_out += lax.dot_general(hid, g, TN, preferred_element_type=F32)
        w_in, w_out = w_in.astype(BF), w_out.astype(BF)
        for t in range(2):
            for half in range(2):
                inner = jnp.bitwise_xor(second, 2 * t + half)
                rows = slice(half * 128, (half + 1) * 128)
                out_ref[jnp.bitwise_xor(first, c), inner] = w_in[rows, t * TILE : (t + 1) * TILE]
                rows = slice(t * TILE + half * 128, t * TILE + (half + 1) * 128)
                out_ref[jnp.bitwise_xor(first, 2 + c), inner] = w_out[rows]


def backward(mine, *args):
    return in_vmem(
        functools.partial(back_kernel, mine), "backward", 3 * ROWS * E * H, [((4, 4, 128, TILE), BF)], *args
    )[0]


def finish_kernel(mine, x_ref, *rest):
    w_in_hbm, w_out_hbm, a, b, sems = rest[-5:]
    core, first, second = order()
    if not mine:
        core, first, second = 1 - core, second, first
    copies = []
    for c in range(2):
        for t in range(2):
            for half in range(2):
                inner = jnp.bitwise_xor(second, 2 * t + half)
                start_t = c * WIDE + t * TILE
                cols = slice(start_t, start_t + TILE)
                a[half * 128 : (half + 1) * 128, cols] = x_ref[jnp.bitwise_xor(first, c), inner].astype(F32)
                rows = slice(start_t + half * 128, start_t + (half + 1) * 128)
                b[rows] = x_ref[jnp.bitwise_xor(first, 2 + c), inner].astype(F32)
        here = pl.ds(c * WIDE, WIDE)
        there = pl.ds(pl.multiple_of(core * (H // 2) + c * WIDE, WIDE), WIDE)
        copies.append(start(a.at[:, here], w_in_hbm.at[:, there], sems.at[2 * c]))
        copies.append(start(b.at[here], w_out_hbm.at[there], sems.at[2 * c + 1]))
    for copy in copies:
        copy.wait()


def finish(mine, x, *outs):
    vm, hbm = pl.BlockSpec(memory_space=pltpu.VMEM), pl.BlockSpec(memory_space=pl.ANY)
    return pl.pallas_call(
        functools.partial(finish_kernel, mine),
        in_specs=[vm] + [hbm] * len(outs),
        out_specs=[hbm, hbm],
        out_shape=[jax.ShapeDtypeStruct((E, H), F32), jax.ShapeDtypeStruct((H, E), F32)],
        scratch_shapes=[
            pltpu.VMEM((E, H // 2), F32),
            pltpu.VMEM((H // 2, E), F32),
            pltpu.SemaphoreType.DMA((4,)),
        ],
        input_output_aliases={1: 0, 2: 1} if outs else {},
        compiler_params=params(14 * 1024 * 1024),
        cost_estimate=cost(0, 3e6),
        name="finish",
    )(x, *outs)


def swap(x, axis, k):
    return lax.ppermute(x, axis, [(i, i ^ k) for i in range(SIZES[AXES.index(axis)])])


def after(x, *needed):
    return lax.optimization_barrier((x, *needed))[0]


def shift(x, by):
    return lax.ppermute(x, "z", [(i, (i + by) % NZ) for i in range(NZ)])


def device(x_lo, z, x_hi, y, core):
    return (((x_lo * 8 + z) * 2 + x_hi) * 4 + y) * 2 + core


def near(place):
    return place ^ (place >> 1)


def plane_swap(x, k, x_core):
    pairs = []
    for z in range(8):
        for xx in range(4):
            for y in range(4):
                for core in range(2):
                    to_x, to_y = (near(near(xx) ^ k), y) if core == x_core else (xx, near(near(y) ^ k))
                    pairs.append(
                        (device(xx & 1, z, xx >> 1, y, core), device(to_x & 1, z, to_x >> 1, to_y, core))
                    )
    return lax.ppermute(x, AXES, pairs)


def add(*terms):
    return sum(t.astype(F32) for t in terms)


def sum_over_z(x, rounds, dtype):
    for ks in rounds:
        sent = x.astype(dtype)
        terms = [t.astype(F32) for t in [sent] + [swap(sent, "z", k) for k in ks]]
        while len(terms) > 1:
            terms = [a + b for a, b in zip(terms[::2], terms[1::2])]
        x = terms[0]
    return x


def gathered(x, x_core, *beside):
    got = {k: plane_swap(x, k, x_core) for k in (1, 2, 3)}
    if beside:
        got, beside = lax.optimization_barrier((got, beside))
    got = jnp.stack([x] + [got[k] for k in (1, 2, 3)])
    return (got, *beside) if beside else got


def all_reduce(mine, theirs, keep, send):
    half = add(mine, swap(theirs, "core", 1)).astype(BF)
    quarter = add(half[0], *[plane_swap(half[k], k, 0) for k in ORDER]).astype(BF)
    keep = add(keep, swap(send, "z", 1)).astype(BF)
    got = [plane_swap(quarter[k], k, 1) for k in ORDER[::-1]]
    got, keep = lax.optimization_barrier((got, keep))
    part = add(quarter[0], *got)
    part = sum_over_z(part, ((1, 7, 6), (2,)), BF).astype(BF)
    part, keep = lax.optimization_barrier((part, keep))
    quarter = gathered(part, 1)
    user = add(keep[0], *[swap(keep[i], "z", k) for i, k in ((1, 4), (2, 2), (3, 6))])
    half, user = gathered(quarter, 0, user)
    return half, swap(half, "core", 1), user


def on_device(user_emb, pos_feat, pos_id, neg_feat, neg_id, neg_bucket, logq_table, w_in, w_out):
    mine, near = pack(user_emb, pos_id, neg_feat, neg_id, neg_bucket)
    up, down = shift(mine, 1), shift(mine, -1)
    far = swap(near, "x_lo", 1)
    users = [mine, up, down]
    hid, feat, w_in = in_vmem(
        hidden_kernel,
        "hidden",
        2 * (N + U) * E * H,
        [((N + U, H), BF), ((N + U, E), BF), ((E, H), BF)],
        neg_feat,
        pos_feat,
        w_in,
    )
    up, down = shift(after(up, hid), 1), shift(after(down, hid), -1)
    users += [up, down]
    near_emb, pemb, w_out = in_vmem(
        embed_kernel, "embed", 2 * (N + U) * E * H, [((N, E), BF), ((U, E), BF), ((H, E), BF)], hid, w_out
    )
    up, down = shift(after(up, near_emb), 1), shift(after(down, near_emb), -1)
    users += [up, down]
    far_hid, far_emb, nid, bias = in_vmem(
        far_kernel,
        "far",
        4 * N * E * H,
        [((N, H), BF), ((N, E), BF), ((NN, 128), F32), ((NN, 128), F32)],
        near,
        far,
        w_in,
        w_out,
        logq_table.reshape(8, 128),
    )
    users += [shift(after(up, far_emb), 1)]
    none = jnp.zeros((NZ, U), F32)
    ks = tuple(range(NZ))
    tloc, tot, pexp, kept_a = score(ks[:FIRST], near_emb, far_emb, nid, bias, pemb, none, none, users)
    tloc, tot, _, kept_b = score(ks[FIRST:], near_emb, far_emb, nid, bias, pemb, tloc, tot, users)
    tot = sum_over_z(tot, ((1, 6, 7), (2,)), F32)
    g = item_grads(tot, tloc, pexp, kept_a, kept_b, users)
    keep, send, pterm = user_grads(tot, tloc, pexp, kept_a, kept_b, near_emb, far_emb, pemb)
    args = (g, feat, far, w_out, hid, far_hid)
    theirs_g = backward(False, *args)
    half, other, user = all_reduce(backward(True, *args), theirs_g, keep, send)
    w_in_grad, w_out_grad = finish(False, other, *finish(True, half))
    return user + pterm, w_in_grad, w_out_grad


def solution(mesh):
    rows = P(AXES, None)
    ids = P(AXES)
    return jax.shard_map(
        on_device,
        mesh=Mesh(mesh.devices.reshape(SIZES), AXES),
        in_specs=(rows, rows, ids, rows, ids, ids, P(), P(), P()),
        out_specs=(rows, P(), P()),
        check_vma=False,
    )
```

profile of v0, /device:TPU:1, one launch (start us, length us, event | category | flops | bytes accessed | tf_op | source)
XLA Modules:
  0.0 117.5 jit_solution(12498291320210586854)
XLA Ops:
  0.7 2.0 %pack.1 = (bf16[272,256]{1,0:T(8,128)(2,1)}, bf16[528,256]{1,0:T(8,128)(2,1)}) custom-call(bf16[256,256]{1,0:T(8,128)(2,1)} %user_hbm.1, s32[1,256]{1,0:T(1,128)} %bitcast.54, bf16[512,256]{1,0:T(8,128)(2,1)} %feat_hbm.1, s32[1,512]{1,0:T(1,128)} %bitcast.52, s32[1,512]{1,0:T(1,128)} %bitcast.53), custom_call_target="tpu_custom_call" | custom-call | flops 10000000000 | bytes 1000000 | tf_op jit(solution)/shard_map/pack/pallas_call | solution.py:83
  2.6 2.5 %collective-permute-start.1 = (bf16[272,256]{1,0:T(8,128)(2,1)}, bf16[272,256]{1,0:T(8,128)(2,1)S(1)}, u32[]{:S(2)}, u32[]{:S(2)}) collective-permute-start(bf16[272,256]{1,0:T(8,128)(2,1)} %get-tuple-element.53.rest_0_), channel_id=1, source_target_pairs={{0,16},{16,32},{32,48},{48,64},{64,80},{80,96},{96,112},{112,0},{1... | collective-permute-start | bytes 417800 | tf_op jit(solution)/shard_map/ppermute | solution.py:363
  5.2 4.0 %collective-permute-start.2 = (bf16[272,256]{1,0:T(8,128)(2,1)}, bf16[272,256]{1,0:T(8,128)(2,1)S(1)}, u32[]{:S(2)}, u32[]{:S(2)}) collective-permute-start(bf16[272,256]{1,0:T(8,128)(2,1)} %get-tuple-element.53.rest_0_), channel_id=1, source_target_pairs={{0,112},{16,0},{32,16},{48,32},{64,48},{80,64},{96,80},{112,96},{1... | collective-permute-start | bytes 417800 | tf_op jit(solution)/shard_map/ppermute | solution.py:363
  12.7 2.7 %collective-permute-start.4 = (bf16[272,256]{1,0:T(8,128)(2,1)S(1)}, bf16[272,256]{1,0:T(8,128)(2,1)S(1)}, u32[]{:S(2)}, u32[]{:S(2)}) collective-permute-start(bf16[272,256]{1,0:T(8,128)(2,1)S(1)} %collective-permute-done.2.rest_2_), channel_id=1, source_target_pairs={{0,112},{16,0},{32,16},{48,32},{64,48},{80,64},{96,80},{112,96},{1... | collective-permute-start | bytes 417800 | tf_op jit(solution)/shard_map/ppermute | solution.py:363
  17.9 2.7 %collective-permute-start.6 = (bf16[272,256]{1,0:T(8,128)(2,1)S(1)}, bf16[272,256]{1,0:T(8,128)(2,1)S(1)}, u32[]{:S(2)}, u32[]{:S(2)}) collective-permute-start(bf16[272,256]{1,0:T(8,128)(2,1)S(1)} %collective-permute-done.4.rest_4_), channel_id=1, source_target_pairs={{0,112},{16,0},{32,16},{48,32},{64,48},{80,64},{96,80},{112,96},{1... | collective-permute-start | bytes 417800 | tf_op jit(solution)/shard_map/ppermute | solution.py:363
  20.5 1.7 %far.1 = (bf16[512,2048]{1,0:T(8,128)(2,1)S(1)}, bf16[512,256]{1,0:T(8,128)(2,1)S(1)}, f32[1024,128]{1,0:T(8,128)S(1)}, f32[1024,128]{1,0:T(8,128)S(1)}) custom-call(bf16[528,256]{1,0:T(8,128)(2,1)S(1)} %copy-done.3, bf16[528,256]{1,0:T(8,128)(2,1)S(1)} %collective-permute-done.far_ref, bf16[256,2048]{1,0:T(8,128)(2,1)S(1)} %get-tuple-element.47.w_in_ref, ...), custom_call_target="tpu_custom_call" | custom-call | flops 1073741824 | bytes 4000000 | tf_op jit(solution)/shard_map/far/pallas_call | solution.py:141
  23.0 3.7 %score.2 = (f32[8,256]{1,0:T(8,128)S(1)}, f32[8,256]{1,0:T(8,128)S(1)}, f32[1,256]{1,0:T(1,128)S(1)}, bf16[1024,1792]{1,0:T(8,128)(2,1)S(1)}) custom-call(bf16[512,256]{1,0:T(8,128)(2,1)S(1)} %get-tuple-element.45.near_emb, bf16[512,256]{1,0:T(8,128)(2,1)S(1)} %get-tuple-element.49.far_emb, f32[1024,128]{1,0:T(8,128)S(1)} %get-tuple-element.50.nid_ref, ...), custom_call_target="tpu_custom_call" | custom-call | flops 939524096 | bytes 5000000 | tf_op jit(solution)/shard_map/score/pallas_call | solution.py:201
  31.2 1.8 %collective-permute-start.8 = (f32[8,256]{1,0:T(8,128)S(1)}, f32[8,256]{1,0:T(8,128)S(1)}, u32[]{:S(2)}, u32[]{:S(2)}) collective-permute-start(f32[8,256]{1,0:T(8,128)S(1)} %get-tuple-element.61), channel_id=1, source_target_pairs={{0,16},{16,0},{32,48},{48,32},{64,80},{80,64},{96,112},{112,96},{1... | collective-permute-start | bytes 24584 | tf_op jit(solution)/shard_map/ppermute | solution.py:355
  33.0 2.0 %collective-permute-done.9 = f32[8,256]{1,0:T(8,128)S(1)} collective-permute-done((f32[8,256]{1,0:T(8,128)S(1)}, f32[8,256]{1,0:T(8,128)S(1)}, u32[]{:S(2)}, u32[]{:S(2)}) %collective-permute-start.9) | collective-permute-done | bytes 8224 | tf_op jit(solution)/shard_map/ppermute | solution.py:355
  35.1 1.9 %collective-permute-start.11 = (f32[8,256]{1,0:T(8,128)S(1)}, f32[8,256]{1,0:T(8,128)S(1)}, u32[]{:S(2)}, u32[]{:S(2)}) collective-permute-start(f32[8,256]{1,0:T(8,128)S(1)} %add_add_fusion), channel_id=1, source_target_pairs={{0,32},{16,48},{32,0},{48,16},{64,96},{80,112},{96,64},{112,80},{1... | collective-permute-start | bytes 24584 | tf_op jit(solution)/shard_map/ppermute | solution.py:355
  36.9 1.6 %collective-permute-done.11 = f32[8,256]{1,0:T(8,128)S(1)} collective-permute-done((f32[8,256]{1,0:T(8,128)S(1)}, f32[8,256]{1,0:T(8,128)S(1)}, u32[]{:S(2)}, u32[]{:S(2)}) %collective-permute-start.11) | collective-permute-done | bytes 8224 | tf_op jit(solution)/shard_map/ppermute | solution.py:355
  38.5 1.5 %items.1.g_ref = bf16[1280,256]{1,0:T(8,128)(2,1)S(1)} custom-call(f32[8,256]{1,0:T(8,128)S(1)} %add.63.tot_ref, f32[8,256]{1,0:T(8,128)S(1)} %get-tuple-element.62.tloc_ref, f32[1,256]{1,0:T(1,128)S(1)} %get-tuple-element.63.pexp_ref, bf16[1024,1792]{1,0:T(8,128)(2,1)S(1)} %get-tuple-element.64.kept_a, bf16[1024,256]{1,0:T(8,128)(2,1)S(1)} %get-tuple-element.65.kept_b, ...), custom_call_target="tpu_custom_call" | custom-call | flops 1073741824 | bytes 4000000 | tf_op jit(solution)/shard_map/items/pallas_call | solution.py:141
  40.1 3.1 %backward.3 = bf16[4,4,128,256]{3,2,1,0:T(8,128)(2,1)S(1)} custom-call(bf16[1280,256]{1,0:T(8,128)(2,1)S(1)} %items.1.g_ref, bf16[768,256]{1,0:T(8,128)(2,1)S(1)} %get-tuple-element.66.feat_ref, bf16[528,256]{1,0:T(8,128)(2,1)S(1)} %collective-permute-done.far_ref, bf16[2048,256]{1,0:T(8,128)(2,1)S(1)} %get-tuple-element.48.w_out_ref, ...), custom_call_target="tpu_custom_call" | custom-call | flops 2013265920 | bytes 4000000 | tf_op jit(solution)/shard_map/backward/pallas_call | solution.py:141
  43.2 6.7 %collective-permute-start.12 = (bf16[4,4,128,256]{3,2,1,0:T(8,128)(2,1)S(1)}, bf16[4,4,128,256]{3,2,1,0:T(8,128)(2,1)S(1)}, u32[]{:S(2)}, u32[]{:S(2)}) collective-permute-start(bf16[4,4,128,256]{3,2,1,0:T(8,128)(2,1)S(1)} %backward.3), channel_id=1, source_target_pairs={{0,1},{1,0},{2,3},{3,2},{4,5},{5,4},{6,7},{7,6},{8,9},{9,8},{10,11... | collective-permute-start | bytes 3145736 | tf_op jit(solution)/shard_map/ppermute | solution.py:355
  49.9 3.1 %backward.2 = bf16[4,4,128,256]{3,2,1,0:T(8,128)(2,1)S(1)} custom-call(bf16[1280,256]{1,0:T(8,128)(2,1)S(1)} %items.1.g_ref, bf16[768,256]{1,0:T(8,128)(2,1)S(1)} %get-tuple-element.66.feat_ref, bf16[528,256]{1,0:T(8,128)(2,1)S(1)} %collective-permute-done.far_ref, bf16[2048,256]{1,0:T(8,128)(2,1)S(1)} %get-tuple-element.48.w_out_ref, ...), custom_call_target="tpu_custom_call" | custom-call | flops 2013265920 | bytes 4000000 | tf_op jit(solution)/shard_map/backward/pallas_call | solution.py:141
  53.4 3.0 %collective-permute-start.13 = (bf16[4,128,256]{2,1,0:T(8,128)(2,1)S(1)}, bf16[4,128,256]{2,1,0:T(8,128)(2,1)S(1)}, u32[]{:S(2)}, u32[]{:S(2)}) collective-permute-start(bf16[4,128,256]{2,1,0:T(8,128)(2,1)S(1)} %get-tuple-element.85), channel_id=1, source_target_pairs={{0,8},{1,5},{2,10},{3,7},{4,12},{5,1},{6,14},{7,3},{128,136},{129,... | collective-permute-start | bytes 786440 | tf_op jit(solution)/shard_map/ppermute | solution.py:384
  57.2 1.6 %users.1 = (bf16[4,256,256]{2,1,0:T(8,128)(2,1)S(1)}, bf16[4,256,256]{2,1,0:T(8,128)(2,1)S(1)}, f32[256,256]{1,0:T(8,128)S(1)}) custom-call(f32[8,256]{1,0:T(8,128)S(1)} %add.63.tot_ref, f32[8,256]{1,0:T(8,128)S(1)} %get-tuple-element.62.tloc_ref, f32[1,256]{1,0:T(1,128)S(1)} %get-tuple-element.63.pexp_ref, bf16[1024,1792]{1,0:T(8,128)(2,1)S(1)} %get-tuple-element.64.kept_a, ...), custom_call_target="tpu_custom_call" | custom-call | flops 1073741824 | bytes 4000000 | tf_op jit(solution)/shard_map/users/pallas_call | solution.py:141
  58.9 1.7 %collective-permute-start.19 = (bf16[4,256,256]{2,1,0:T(8,128)(2,1)S(1)}, bf16[4,256,256]{2,1,0:T(8,128)(2,1)S(1)}, u32[]{:S(2)}, u32[]{:S(2)}) collective-permute-start(bf16[4,256,256]{2,1,0:T(8,128)(2,1)S(1)} %get-tuple-element.69), channel_id=1, source_target_pairs={{0,16},{16,0},{32,48},{48,32},{64,80},{80,64},{96,112},{112,96},{1... | collective-permute-start | bytes 1572872 | tf_op jit(solution)/shard_map/ppermute | solution.py:355
  60.6 3.2 %collective-permute-done.15 = bf16[4,128,256]{2,1,0:T(8,128)(2,1)S(1)} collective-permute-done((bf16[4,128,256]{2,1,0:T(8,128)(2,1)S(1)}, bf16[4,128,256]{2,1,0:T(8,128)(2,1)S(1)}, u32[]{:S(2)}, u32[]{:S(2)}) %collective-permute-start.15) | collective-permute-done | bytes 262176 | tf_op jit(solution)/shard_map/ppermute | solution.py:384
  63.9 2.8 %collective-permute-start.18 = (bf16[128,256]{1,0:T(8,128)(2,1)S(1)}, bf16[128,256]{1,0:T(8,128)(2,1)S(1)}, u32[]{:S(2)}, u32[]{:S(2)}) collective-permute-start(bf16[128,256]{1,0:T(8,128)(2,1)S(1)} %get-tuple-element.93), channel_id=1, source_target_pairs={{0,4},{1,9},{2,6},{3,11},{4,0},{5,13},{6,2},{7,15},{128,132},{129,... | collective-permute-start | bytes 196616 | tf_op jit(solution)/shard_map/ppermute | solution.py:384
  67.6 4.7 %collective-permute-done.19 = bf16[4,256,256]{2,1,0:T(8,128)(2,1)S(1)} collective-permute-done((bf16[4,256,256]{2,1,0:T(8,128)(2,1)S(1)}, bf16[4,256,256]{2,1,0:T(8,128)(2,1)S(1)}, u32[]{:S(2)}, u32[]{:S(2)}) %collective-permute-start.19) | collective-permute-done | bytes 524320 | tf_op jit(solution)/shard_map/ppermute | solution.py:355
  72.5 2.1 %collective-permute-start.22 = (bf16[128,256]{1,0:T(8,128)(2,1)S(1)}, bf16[128,256]{1,0:T(8,128)(2,1)S(1)}, u32[]{:S(2)}, u32[]{:S(2)}) collective-permute-start(bf16[128,256]{1,0:T(8,128)(2,1)S(1)} %fusion.7), channel_id=1, source_target_pairs={{0,96},{16,112},{32,64},{48,80},{64,32},{80,48},{96,0},{112,16},{1... | collective-permute-start | bytes 196616 | tf_op jit(solution)/shard_map/ppermute | solution.py:355
  74.6 1.7 %collective-permute-start.21 = (bf16[128,256]{1,0:T(8,128)(2,1)S(1)}, bf16[128,256]{1,0:T(8,128)(2,1)S(1)}, u32[]{:S(2)}, u32[]{:S(2)}) collective-permute-start(bf16[128,256]{1,0:T(8,128)(2,1)S(1)} %fusion.7), channel_id=1, source_target_pairs={{0,112},{16,96},{32,80},{48,64},{64,48},{80,32},{96,16},{112,0},{1... | collective-permute-start | bytes 196616 | tf_op jit(solution)/shard_map/ppermute | solution.py:355
  77.9 3.1 %collective-permute-done.21 = bf16[128,256]{1,0:T(8,128)(2,1)S(1)} collective-permute-done((bf16[128,256]{1,0:T(8,128)(2,1)S(1)}, bf16[128,256]{1,0:T(8,128)(2,1)S(1)}, u32[]{:S(2)}, u32[]{:S(2)}) %collective-permute-start.21) | collective-permute-done | bytes 65568 | tf_op jit(solution)/shard_map/ppermute | solution.py:355
  81.0 3.2 %collective-permute-start.23 = (bf16[128,256]{1,0:T(8,128)(2,1)S(1)}, bf16[128,256]{1,0:T(8,128)(2,1)S(1)}, u32[]{:S(2)}, u32[]{:S(2)}) collective-permute-start(bf16[128,256]{1,0:T(8,128)(2,1)S(1)} %add_convert_fusion.3), channel_id=1, source_target_pairs={{0,32},{16,48},{32,0},{48,16},{64,96},{80,112},{96,64},{112,80},{1... | collective-permute-start | bytes 196616 | tf_op jit(solution)/shard_map/ppermute | solution.py:355
  84.2 2.4 %collective-permute-done.23 = bf16[128,256]{1,0:T(8,128)(2,1)S(1)} collective-permute-done((bf16[128,256]{1,0:T(8,128)(2,1)S(1)}, bf16[128,256]{1,0:T(8,128)(2,1)S(1)}, u32[]{:S(2)}, u32[]{:S(2)}) %collective-permute-start.23) | collective-permute-done | bytes 65568 | tf_op jit(solution)/shard_map/ppermute | solution.py:355
  86.6 2.1 %collective-permute-start.26 = (bf16[128,256]{1,0:T(8,128)(2,1)S(1)}, bf16[128,256]{1,0:T(8,128)(2,1)S(1)}, u32[]{:S(2)}, u32[]{:S(2)}) collective-permute-start(bf16[128,256]{1,0:T(8,128)(2,1)S(1)} %add_convert_fusion.2), channel_id=1, source_target_pairs={{0,4},{1,9},{2,6},{3,11},{4,0},{5,13},{6,2},{7,15},{128,132},{129,... | collective-permute-start | bytes 196616 | tf_op jit(solution)/shard_map/ppermute | solution.py:384
  89.6 4.3 %collective-permute-start.30 = (bf16[256,256]{1,0:T(8,128)(2,1)S(1)}, bf16[256,256]{1,0:T(8,128)(2,1)S(1)}, u32[]{:S(2)}, u32[]{:S(2)}) collective-permute-start(bf16[256,256]{1,0:T(8,128)(2,1)S(1)} %get-tuple-element.88), channel_id=1, source_target_pairs={{0,64},{16,80},{32,96},{48,112},{64,0},{80,16},{96,32},{112,48},{1... | collective-permute-start | bytes 393224 | tf_op jit(solution)/shard_map/ppermute | solution.py:355
  93.9 1.6 %collective-permute-start.32 = (bf16[256,256]{1,0:T(8,128)(2,1)S(1)}, bf16[256,256]{1,0:T(8,128)(2,1)S(1)}, u32[]{:S(2)}, u32[]{:S(2)}) collective-permute-start(bf16[256,256]{1,0:T(8,128)(2,1)S(1)} %get-tuple-element.89), channel_id=1, source_target_pairs={{0,96},{16,112},{32,64},{48,80},{64,32},{80,48},{96,0},{112,16},{1... | collective-permute-start | bytes 393224 | tf_op jit(solution)/shard_map/ppermute | solution.py:355
  95.5 2.8 %collective-permute-start.29 = (bf16[4,128,256]{2,1,0:T(8,128)(2,1)S(1)}, bf16[4,128,256]{2,1,0:T(8,128)(2,1)S(1)}, u32[]{:S(2)}, u32[]{:S(2)}) collective-permute-start(bf16[4,128,256]{2,1,0:T(8,128)(2,1)S(1)} %get-tuple-element.92), channel_id=1, source_target_pairs={{0,8},{1,5},{2,10},{3,7},{4,12},{5,1},{6,14},{7,3},{128,136},{129,... | collective-permute-start | bytes 786440 | tf_op jit(solution)/shard_map/ppermute | solution.py:384
  99.6 3.6 %collective-permute-done.32 = bf16[256,256]{1,0:T(8,128)(2,1)S(1)} collective-permute-done((bf16[256,256]{1,0:T(8,128)(2,1)S(1)}, bf16[256,256]{1,0:T(8,128)(2,1)S(1)}, u32[]{:S(2)}, u32[]{:S(2)}) %collective-permute-start.32) | collective-permute-done | bytes 131104 | tf_op jit(solution)/shard_map/ppermute | solution.py:355
  105.8 7.9 %collective-permute-start.33 = (bf16[4,4,128,256]{3,2,1,0:T(8,128)(2,1)S(1)}, bf16[4,4,128,256]{3,2,1,0:T(8,128)(2,1)S(1)}, u32[]{:S(2)}, u32[]{:S(2)}) collective-permute-start(bf16[4,4,128,256]{3,2,1,0:T(8,128)(2,1)S(1)} %pad_maximum_fusion.x_ref), channel_id=1, source_target_pairs={{0,1},{1,0},{2,3},{3,2},{4,5},{5,4},{6,7},{7,6},{8,9},{9,8},{10,11... | collective-permute-start | bytes 3145736 | tf_op jit(solution)/shard_map/ppermute | solution.py:355
  (78 shorter events, 23.7 us)
Async XLA Ops:
  2.6 10.1 %collective-permute-start.1 = (bf16[272,256]{1,0:T(8,128)(2,1)}, bf16[272,256]{1,0:T(8,128)(2,1)S(1)}, u32[]{:S(2)}, u32[]{:S(2)}) collective-permute-start(bf16[272,256]{1,0:T(8,128)(2,1)} %get-tuple-element.53.rest_0_), channel_id=1, source_target_pairs={{0,16},{16,32},{32,48},{48,64},{64,80},{80,96},{96,112},{112,0},{1... | collective-permute-start | bytes 417800 | tf_op jit(solution)/shard_map/ppermute | solution.py:363
  5.2 7.6 %collective-permute-start.2 = (bf16[272,256]{1,0:T(8,128)(2,1)}, bf16[272,256]{1,0:T(8,128)(2,1)S(1)}, u32[]{:S(2)}, u32[]{:S(2)}) collective-permute-start(bf16[272,256]{1,0:T(8,128)(2,1)} %get-tuple-element.53.rest_0_), channel_id=1, source_target_pairs={{0,112},{16,0},{32,16},{48,32},{64,48},{80,64},{96,80},{112,96},{1... | collective-permute-start | bytes 417800 | tf_op jit(solution)/shard_map/ppermute | solution.py:363
  9.2 11.3 %collective-permute-start = (bf16[528,256]{1,0:T(8,128)(2,1)}, bf16[528,256]{1,0:T(8,128)(2,1)S(1)}, u32[]{:S(2)}, u32[]{:S(2)}) collective-permute-start(bf16[528,256]{1,0:T(8,128)(2,1)} %get-tuple-element.46.near_ref), channel_id=1, source_target_pairs={{0,128},{128,0},{1,129},{129,1},{2,130},{130,2},{3,131},{131,3},{4... | collective-permute-start | bytes 811016 | tf_op jit(solution)/shard_map/ppermute | solution.py:355
  12.7 5.1 %collective-permute-start.3 = (bf16[272,256]{1,0:T(8,128)(2,1)S(1)}, bf16[272,256]{1,0:T(8,128)(2,1)S(1)}, u32[]{:S(2)}, u32[]{:S(2)}) collective-permute-start(bf16[272,256]{1,0:T(8,128)(2,1)S(1)} %collective-permute-done.1.rest_1_), channel_id=1, source_target_pairs={{0,16},{16,32},{32,48},{48,64},{64,80},{80,96},{96,112},{112,0},{1... | collective-permute-start | bytes 417800 | tf_op jit(solution)/shard_map/ppermute | solution.py:363
  12.7 5.1 %collective-permute-start.4 = (bf16[272,256]{1,0:T(8,128)(2,1)S(1)}, bf16[272,256]{1,0:T(8,128)(2,1)S(1)}, u32[]{:S(2)}, u32[]{:S(2)}) collective-permute-start(bf16[272,256]{1,0:T(8,128)(2,1)S(1)} %collective-permute-done.2.rest_2_), channel_id=1, source_target_pairs={{0,112},{16,0},{32,16},{48,32},{64,48},{80,64},{96,80},{112,96},{1... | collective-permute-start | bytes 417800 | tf_op jit(solution)/shard_map/ppermute | solution.py:363
  17.9 5.1 %collective-permute-start.5 = (bf16[272,256]{1,0:T(8,128)(2,1)S(1)}, bf16[272,256]{1,0:T(8,128)(2,1)S(1)}, u32[]{:S(2)}, u32[]{:S(2)}) collective-permute-start(bf16[272,256]{1,0:T(8,128)(2,1)S(1)} %collective-permute-done.3.rest_3_), channel_id=1, source_target_pairs={{0,16},{16,32},{32,48},{48,64},{64,80},{80,96},{96,112},{112,0},{1... | collective-permute-start | bytes 417800 | tf_op jit(solution)/shard_map/ppermute | solution.py:363
  17.9 5.1 %collective-permute-start.6 = (bf16[272,256]{1,0:T(8,128)(2,1)S(1)}, bf16[272,256]{1,0:T(8,128)(2,1)S(1)}, u32[]{:S(2)}, u32[]{:S(2)}) collective-permute-start(bf16[272,256]{1,0:T(8,128)(2,1)S(1)} %collective-permute-done.4.rest_4_), channel_id=1, source_target_pairs={{0,112},{16,0},{32,16},{48,32},{64,48},{80,64},{96,80},{112,96},{1... | collective-permute-start | bytes 417800 | tf_op jit(solution)/shard_map/ppermute | solution.py:363
  23.0 5.1 %collective-permute-start.7 = (bf16[272,256]{1,0:T(8,128)(2,1)S(1)}, bf16[272,256]{1,0:T(8,128)(2,1)S(1)}, u32[]{:S(2)}, u32[]{:S(2)}) collective-permute-start(bf16[272,256]{1,0:T(8,128)(2,1)S(1)} %collective-permute-done.5.rest_5_), channel_id=1, source_target_pairs={{0,16},{16,32},{32,48},{48,64},{64,80},{80,96},{96,112},{112,0},{1... | collective-permute-start | bytes 417800 | tf_op jit(solution)/shard_map/ppermute | solution.py:363
  29.2 3.9 %collective-permute-start.10 = (f32[8,256]{1,0:T(8,128)S(1)}, f32[8,256]{1,0:T(8,128)S(1)}, u32[]{:S(2)}, u32[]{:S(2)}) collective-permute-start(f32[8,256]{1,0:T(8,128)S(1)} %get-tuple-element.61), channel_id=1, source_target_pairs={{0,112},{16,96},{32,80},{48,64},{64,48},{80,32},{96,16},{112,0},{1... | collective-permute-start | bytes 24584 | tf_op jit(solution)/shard_map/ppermute | solution.py:355
  30.4 4.6 %collective-permute-start.9 = (f32[8,256]{1,0:T(8,128)S(1)}, f32[8,256]{1,0:T(8,128)S(1)}, u32[]{:S(2)}, u32[]{:S(2)}) collective-permute-start(f32[8,256]{1,0:T(8,128)S(1)} %get-tuple-element.61), channel_id=1, source_target_pairs={{0,96},{16,112},{32,64},{48,80},{64,32},{80,48},{96,0},{112,16},{1... | collective-permute-start | bytes 24584 | tf_op jit(solution)/shard_map/ppermute | solution.py:355
  43.2 9.8 %collective-permute-start.12 = (bf16[4,4,128,256]{3,2,1,0:T(8,128)(2,1)S(1)}, bf16[4,4,128,256]{3,2,1,0:T(8,128)(2,1)S(1)}, u32[]{:S(2)}, u32[]{:S(2)}) collective-permute-start(bf16[4,4,128,256]{3,2,1,0:T(8,128)(2,1)S(1)} %backward.3), channel_id=1, source_target_pairs={{0,1},{1,0},{2,3},{3,2},{4,5},{5,4},{6,7},{7,6},{8,9},{9,8},{10,11... | collective-permute-start | bytes 3145736 | tf_op jit(solution)/shard_map/ppermute | solution.py:355
  53.4 7.1 %collective-permute-start.13 = (bf16[4,128,256]{2,1,0:T(8,128)(2,1)S(1)}, bf16[4,128,256]{2,1,0:T(8,128)(2,1)S(1)}, u32[]{:S(2)}, u32[]{:S(2)}) collective-permute-start(bf16[4,128,256]{2,1,0:T(8,128)(2,1)S(1)} %get-tuple-element.85), channel_id=1, source_target_pairs={{0,8},{1,5},{2,10},{3,7},{4,12},{5,1},{6,14},{7,3},{128,136},{129,... | collective-permute-start | bytes 786440 | tf_op jit(solution)/shard_map/ppermute | solution.py:384
  56.5 7.3 %collective-permute-start.15 = (bf16[4,128,256]{2,1,0:T(8,128)(2,1)S(1)}, bf16[4,128,256]{2,1,0:T(8,128)(2,1)S(1)}, u32[]{:S(2)}, u32[]{:S(2)}) collective-permute-start(bf16[4,128,256]{2,1,0:T(8,128)(2,1)S(1)} %get-tuple-element.86), channel_id=1, source_target_pairs={{0,128},{1,3},{2,130},{3,1},{4,132},{5,7},{6,134},{7,5},{128,0},{1... | collective-permute-start | bytes 786440 | tf_op jit(solution)/shard_map/ppermute | solution.py:384
  56.9 6.9 %collective-permute-start.14 = (bf16[4,128,256]{2,1,0:T(8,128)(2,1)S(1)}, bf16[4,128,256]{2,1,0:T(8,128)(2,1)S(1)}, u32[]{:S(2)}, u32[]{:S(2)}) collective-permute-start(bf16[4,128,256]{2,1,0:T(8,128)(2,1)S(1)} %get-tuple-element.87), channel_id=1, source_target_pairs={{0,136},{1,7},{2,138},{3,5},{4,140},{5,3},{6,142},{7,1},{128,8},{1... | collective-permute-start | bytes 786440 | tf_op jit(solution)/shard_map/ppermute | solution.py:384
  58.9 13.5 %collective-permute-start.19 = (bf16[4,256,256]{2,1,0:T(8,128)(2,1)S(1)}, bf16[4,256,256]{2,1,0:T(8,128)(2,1)S(1)}, u32[]{:S(2)}, u32[]{:S(2)}) collective-permute-start(bf16[4,256,256]{2,1,0:T(8,128)(2,1)S(1)} %get-tuple-element.69), channel_id=1, source_target_pairs={{0,16},{16,0},{32,48},{48,32},{64,80},{80,64},{96,112},{112,96},{1... | collective-permute-start | bytes 1572872 | tf_op jit(solution)/shard_map/ppermute | solution.py:355
  63.9 8.5 %collective-permute-start.18 = (bf16[128,256]{1,0:T(8,128)(2,1)S(1)}, bf16[128,256]{1,0:T(8,128)(2,1)S(1)}, u32[]{:S(2)}, u32[]{:S(2)}) collective-permute-start(bf16[128,256]{1,0:T(8,128)(2,1)S(1)} %get-tuple-element.93), channel_id=1, source_target_pairs={{0,4},{1,9},{2,6},{3,11},{4,0},{5,13},{6,2},{7,15},{128,132},{129,... | collective-permute-start | bytes 196616 | tf_op jit(solution)/shard_map/ppermute | solution.py:384
  66.7 5.7 %collective-permute-start.17 = (bf16[128,256]{1,0:T(8,128)(2,1)S(1)}, bf16[128,256]{1,0:T(8,128)(2,1)S(1)}, u32[]{:S(2)}, u32[]{:S(2)}) collective-permute-start(bf16[128,256]{1,0:T(8,128)(2,1)S(1)} %get-tuple-element.94), channel_id=1, source_target_pairs={{0,6},{1,137},{2,4},{3,139},{4,2},{5,141},{6,0},{7,143},{128,134},... | collective-permute-start | bytes 196616 | tf_op jit(solution)/shard_map/ppermute | solution.py:384
  67.6 4.9 %collective-permute-start.16 = (bf16[128,256]{1,0:T(8,128)(2,1)S(1)}, bf16[128,256]{1,0:T(8,128)(2,1)S(1)}, u32[]{:S(2)}, u32[]{:S(2)}) collective-permute-start(bf16[128,256]{1,0:T(8,128)(2,1)S(1)} %get-tuple-element.95), channel_id=1, source_target_pairs={{0,2},{1,129},{2,0},{3,131},{4,6},{5,133},{6,4},{7,135},{128,130},... | collective-permute-start | bytes 196616 | tf_op jit(solution)/shard_map/ppermute | solution.py:384
  72.5 5.4 %collective-permute-start.22 = (bf16[128,256]{1,0:T(8,128)(2,1)S(1)}, bf16[128,256]{1,0:T(8,128)(2,1)S(1)}, u32[]{:S(2)}, u32[]{:S(2)}) collective-permute-start(bf16[128,256]{1,0:T(8,128)(2,1)S(1)} %fusion.7), channel_id=1, source_target_pairs={{0,96},{16,112},{32,64},{48,80},{64,32},{80,48},{96,0},{112,16},{1... | collective-permute-start | bytes 196616 | tf_op jit(solution)/shard_map/ppermute | solution.py:355
  74.6 6.4 %collective-permute-start.21 = (bf16[128,256]{1,0:T(8,128)(2,1)S(1)}, bf16[128,256]{1,0:T(8,128)(2,1)S(1)}, u32[]{:S(2)}, u32[]{:S(2)}) collective-permute-start(bf16[128,256]{1,0:T(8,128)(2,1)S(1)} %fusion.7), channel_id=1, source_target_pairs={{0,112},{16,96},{32,80},{48,64},{64,48},{80,32},{96,16},{112,0},{1... | collective-permute-start | bytes 196616 | tf_op jit(solution)/shard_map/ppermute | solution.py:355
  76.3 4.7 %collective-permute-start.20 = (bf16[128,256]{1,0:T(8,128)(2,1)S(1)}, bf16[128,256]{1,0:T(8,128)(2,1)S(1)}, u32[]{:S(2)}, u32[]{:S(2)}) collective-permute-start(bf16[128,256]{1,0:T(8,128)(2,1)S(1)} %fusion.7), channel_id=1, source_target_pairs={{0,16},{16,0},{32,48},{48,32},{64,80},{80,64},{96,112},{112,96},{1... | collective-permute-start | bytes 196616 | tf_op jit(solution)/shard_map/ppermute | solution.py:355
  81.0 5.5 %collective-permute-start.23 = (bf16[128,256]{1,0:T(8,128)(2,1)S(1)}, bf16[128,256]{1,0:T(8,128)(2,1)S(1)}, u32[]{:S(2)}, u32[]{:S(2)}) collective-permute-start(bf16[128,256]{1,0:T(8,128)(2,1)S(1)} %add_convert_fusion.3), channel_id=1, source_target_pairs={{0,32},{16,48},{32,0},{48,16},{64,96},{80,112},{96,64},{112,80},{1... | collective-permute-start | bytes 196616 | tf_op jit(solution)/shard_map/ppermute | solution.py:355
  86.6 8.9 %collective-permute-start.26 = (bf16[128,256]{1,0:T(8,128)(2,1)S(1)}, bf16[128,256]{1,0:T(8,128)(2,1)S(1)}, u32[]{:S(2)}, u32[]{:S(2)}) collective-permute-start(bf16[128,256]{1,0:T(8,128)(2,1)S(1)} %add_convert_fusion.2), channel_id=1, source_target_pairs={{0,4},{1,9},{2,6},{3,11},{4,0},{5,13},{6,2},{7,15},{128,132},{129,... | collective-permute-start | bytes 196616 | tf_op jit(solution)/shard_map/ppermute | solution.py:384
  88.7 6.7 %collective-permute-start.25 = (bf16[128,256]{1,0:T(8,128)(2,1)S(1)}, bf16[128,256]{1,0:T(8,128)(2,1)S(1)}, u32[]{:S(2)}, u32[]{:S(2)}) collective-permute-start(bf16[128,256]{1,0:T(8,128)(2,1)S(1)} %add_convert_fusion.2), channel_id=1, source_target_pairs={{0,6},{1,137},{2,4},{3,139},{4,2},{5,141},{6,0},{7,143},{128,134},... | collective-permute-start | bytes 196616 | tf_op jit(solution)/shard_map/ppermute | solution.py:384
  89.6 5.9 %collective-permute-start.24 = (bf16[128,256]{1,0:T(8,128)(2,1)S(1)}, bf16[128,256]{1,0:T(8,128)(2,1)S(1)}, u32[]{:S(2)}, u32[]{:S(2)}) collective-permute-start(bf16[128,256]{1,0:T(8,128)(2,1)S(1)} %add_convert_fusion.2), channel_id=1, source_target_pairs={{0,2},{1,129},{2,0},{3,131},{4,6},{5,133},{6,4},{7,135},{128,130},... | collective-permute-start | bytes 196616 | tf_op jit(solution)/shard_map/ppermute | solution.py:384
  89.6 9.5 %collective-permute-start.30 = (bf16[256,256]{1,0:T(8,128)(2,1)S(1)}, bf16[256,256]{1,0:T(8,128)(2,1)S(1)}, u32[]{:S(2)}, u32[]{:S(2)}) collective-permute-start(bf16[256,256]{1,0:T(8,128)(2,1)S(1)} %get-tuple-element.88), channel_id=1, source_target_pairs={{0,64},{16,80},{32,96},{48,112},{64,0},{80,16},{96,32},{112,48},{1... | collective-permute-start | bytes 393224 | tf_op jit(solution)/shard_map/ppermute | solution.py:355
  93.9 9.3 %collective-permute-start.32 = (bf16[256,256]{1,0:T(8,128)(2,1)S(1)}, bf16[256,256]{1,0:T(8,128)(2,1)S(1)}, u32[]{:S(2)}, u32[]{:S(2)}) collective-permute-start(bf16[256,256]{1,0:T(8,128)(2,1)S(1)} %get-tuple-element.89), channel_id=1, source_target_pairs={{0,96},{16,112},{32,64},{48,80},{64,32},{80,48},{96,0},{112,16},{1... | collective-permute-start | bytes 393224 | tf_op jit(solution)/shard_map/ppermute | solution.py:355
  95.5 9.2 %collective-permute-start.31 = (bf16[256,256]{1,0:T(8,128)(2,1)S(1)}, bf16[256,256]{1,0:T(8,128)(2,1)S(1)}, u32[]{:S(2)}, u32[]{:S(2)}) collective-permute-start(bf16[256,256]{1,0:T(8,128)(2,1)S(1)} %get-tuple-element.90), channel_id=1, source_target_pairs={{0,32},{16,48},{32,0},{48,16},{64,96},{80,112},{96,64},{112,80},{1... | collective-permute-start | bytes 393224 | tf_op jit(solution)/shard_map/ppermute | solution.py:355
  95.5 9.2 %collective-permute-start.29 = (bf16[4,128,256]{2,1,0:T(8,128)(2,1)S(1)}, bf16[4,128,256]{2,1,0:T(8,128)(2,1)S(1)}, u32[]{:S(2)}, u32[]{:S(2)}) collective-permute-start(bf16[4,128,256]{2,1,0:T(8,128)(2,1)S(1)} %get-tuple-element.92), channel_id=1, source_target_pairs={{0,8},{1,5},{2,10},{3,7},{4,12},{5,1},{6,14},{7,3},{128,136},{129,... | collective-permute-start | bytes 786440 | tf_op jit(solution)/shard_map/ppermute | solution.py:384
  98.3 7.1 %collective-permute-start.28 = (bf16[4,128,256]{2,1,0:T(8,128)(2,1)S(1)}, bf16[4,128,256]{2,1,0:T(8,128)(2,1)S(1)}, u32[]{:S(2)}, u32[]{:S(2)}) collective-permute-start(bf16[4,128,256]{2,1,0:T(8,128)(2,1)S(1)} %get-tuple-element.92), channel_id=1, source_target_pairs={{0,136},{1,7},{2,138},{3,5},{4,140},{5,3},{6,142},{7,1},{128,8},{1... | collective-permute-start | bytes 786440 | tf_op jit(solution)/shard_map/ppermute | solution.py:384
  99.1 6.5 %collective-permute-start.27 = (bf16[4,128,256]{2,1,0:T(8,128)(2,1)S(1)}, bf16[4,128,256]{2,1,0:T(8,128)(2,1)S(1)}, u32[]{:S(2)}, u32[]{:S(2)}) collective-permute-start(bf16[4,128,256]{2,1,0:T(8,128)(2,1)S(1)} %get-tuple-element.92), channel_id=1, source_target_pairs={{0,128},{1,3},{2,130},{3,1},{4,132},{5,7},{6,134},{7,5},{128,0},{1... | collective-permute-start | bytes 786440 | tf_op jit(solution)/shard_map/ppermute | solution.py:384
  105.8 10.2 %collective-permute-start.33 = (bf16[4,4,128,256]{3,2,1,0:T(8,128)(2,1)S(1)}, bf16[4,4,128,256]{3,2,1,0:T(8,128)(2,1)S(1)}, u32[]{:S(2)}, u32[]{:S(2)}) collective-permute-start(bf16[4,4,128,256]{3,2,1,0:T(8,128)(2,1)S(1)} %pad_maximum_fusion.x_ref), channel_id=1, source_target_pairs={{0,1},{1,0},{2,3},{3,2},{4,5},{5,4},{6,7},{7,6},{8,9},{9,8},{10,11... | collective-permute-start | bytes 3145736 | tf_op jit(solution)/shard_map/ppermute | solution.py:355
  (9 other events, 71.6 us)
where the time goes:
time: 118 us
  starting transfers between devices  63.5 us (54%)
  waiting for transfers between devices  28.4 us (24%)
  Pallas kernels  22.6 us (19%)
  other arithmetic  1.69 us (1%)
    ppermute x15, starting transfers between devices, swap(): lax.ppermute(x, axis, [(i, i ^ k) for i in range(SIZES[AXES.index(axis)])])  37.1 us
    ppermute x15, waiting for transfers between devices, swap(): lax.ppermute(x, axis, [(i, i ^ k) for i in range(SIZES[AXES.index(axis)])])  19.6 us
    ppermute x12, starting transfers between devices, plane_swap(): return lax.ppermute(x, AXES, pairs)  14.5 us
    pallas_call x7, Pallas kernels, in_vmem(): pl.pallas_call(kernel, in_specs=[vm] * len(args), out_specs=[vm] * len(ou...  13.2 us
    ppermute x7, starting transfers between devices, shift(): return lax.ppermute(x, 'z', [(i, (i + by) % NZ) for i in range(NZ)])  11.9 us
    ppermute x7, waiting for transfers between devices, shift(): return lax.ppermute(x, 'z', [(i, (i + by) % NZ) for i in range(NZ)])  4.78 us
    pallas_call x2, Pallas kernels, score(): pl.pallas_call(functools.partial(score_kernel, ks), in_specs=[vm] * (7 +...  4.74 us
    ppermute x12, waiting for transfers between devices, plane_swap(): return lax.ppermute(x, AXES, pairs)  4.1 us
  transfers between devices with their start and end apart: 34, of which 16 were waited for; matrix products, arithmetic and copies ran while one was open for 1% of the time, Pallas kernels for 12%

commit v1 on v0

--- a/solution.py
+++ b/solution.py
@@ -111,9 +111,12 @@
 
 def embed_kernel(hid_ref, w_out_ref, emb_ref, pemb_ref, w_out_out):
     w_out_out[...] = w_out_ref[...]
-    for m, (ref, first) in enumerate([(emb_ref, 0), (emb_ref, TILE), (pemb_ref, 0)]):
-        hid = hid_ref[m * TILE : (m + 1) * TILE]
-        ref[first : first + TILE] = mm(hid, w_out_ref[...]).astype(BF)
+    pemb_ref[...] = mm(hid_ref[N : N + U], w_out_ref[...]).astype(BF)
+
+    @pl.loop(0, N // TILE)
+    def _(m):
+        rows = pl.ds(pl.multiple_of(m * TILE, TILE), TILE)
+        emb_ref[rows, :] = mm(hid_ref[rows, :], w_out_ref[...]).astype(BF)
 
 
 def far_kernel(near_ref, far_ref, w_in_ref, w_out_ref, table_ref, hid_ref, emb_ref, nid_ref, bias_ref):
@@ -129,11 +132,13 @@
             for b in range(8):
                 found = found + jnp.where(bucket == lane + 128.0 * b, table_ref[b : b + 1], 0.0)
             bias_ref[rows] = jnp.broadcast_to(jnp.sum(found, axis=1, keepdims=True), (TILE, 128))
-    for m in range(N // TILE):
-        rows = slice(m * TILE, (m + 1) * TILE)
-        hid = hidden(far_ref[rows], w_in_ref)
-        hid_ref[rows] = hid
-        emb_ref[rows] = mm(hid, w_out_ref[...]).astype(BF)
+
+    @pl.loop(0, N // TILE)
+    def _(m):
+        rows = pl.ds(pl.multiple_of(m * TILE, TILE), TILE)
+        hid = hidden(far_ref[rows, :], w_in_ref)
+        hid_ref[rows, :] = hid
+        emb_ref[rows, :] = mm(hid, w_out_ref[...]).astype(BF)
 
 
 def in_vmem(kernel, name, flops, outs, *args, scratch=()):
@@ -247,19 +252,21 @@
         g_ref[first : first + TILE] = g.astype(BF)
 
 
-def user_grad_kernel(tot_ref, tloc_ref, pexp_ref, kept_a, kept_b, near_emb, far_emb, pemb_ref, *rest):
-    keep_ref, send_ref, pterm_ref, ratio, rel = rest
+def user_grad_kernel(odd, tot_ref, tloc_ref, pexp_ref, kept_a, kept_b, near_emb, far_emb, pemb_ref, out_ref, *rest):
     z = lax.axis_index("z")
-    cols = ratios(tot_ref, tloc_ref, pexp_ref, ratio, rel)
-    pterm_ref[...] = pemb_ref[...].astype(F32) * cols[:, NZ : NZ + 1]
+    cols = ratios(tot_ref, tloc_ref, pexp_ref, *rest[-2:])
+    if not odd:
+        rest[0][...] = pemb_ref[...].astype(F32) * cols[:, NZ : NZ + 1]
     for k in range(NZ):
+        if OFFSETS[k] % 2 != odd:
+            continue
         kept, i = (kept_a, k) if k < FIRST else (kept_b, k - FIRST)
         cols_k = slice(i * U, (i + 1) * U)
         ug = lax.dot_general(kept[0:N, cols_k], near_emb[...], TN, preferred_element_type=F32)
         ug = ug + lax.dot_general(kept[N:NN, cols_k], far_emb[...], TN, preferred_element_type=F32)
         apart = jnp.bitwise_xor(home(z, k), z)
         place = (apart & 2) + (apart >> 2)
-        (send_ref if OFFSETS[k] % 2 else keep_ref)[place] = (ug * cols[:, k : k + 1]).astype(BF)
+        out_ref[place] = (ug * cols[:, k : k + 1]).astype(BF)
 
 
 def item_grads(tot, tloc, pexp, kept_a, kept_b, users):
@@ -268,9 +275,10 @@
     return in_vmem(item_grad_kernel, "items", 2 * NZ * U * NN * E, [((ROWS, E), BF)], *args, scratch=scratch)[0]
 
 
-def user_grads(*args):
-    outs = [((NZ // 2, U, E), BF), ((NZ // 2, U, E), BF), ((U, E), F32)]
-    return in_vmem(user_grad_kernel, "users", 2 * NZ * U * NN * E, outs, *args, scratch=RATIOS)
+def user_grads(odd, *args):
+    outs = [((NZ // 2, U, E), BF)] + ([] if odd else [((U, E), F32)])
+    kernel = functools.partial(user_grad_kernel, odd)
+    return in_vmem(kernel, "users", NZ * U * NN * E, outs, *args, scratch=RATIOS)
 
 
 def order():
@@ -460,7 +468,8 @@
     tloc, tot, _, kept_b = score(ks[FIRST:], near_emb, far_emb, nid, bias, pemb, tloc, tot, users)
     tot = sum_over_z(tot, ((1, 6, 7), (2,)), F32)
     g = item_grads(tot, tloc, pexp, kept_a, kept_b, users)
-    keep, send, pterm = user_grads(tot, tloc, pexp, kept_a, kept_b, near_emb, far_emb, pemb)
+    args = (tot, tloc, pexp, kept_a, kept_b, near_emb, far_emb, pemb)
+    (send,), (keep, pterm) = user_grads(1, *args), user_grads(0, *args)
     args = (g, feat, far, w_out, hid, far_hid)
     theirs_g = backward(False, *args)
     half, other, user = all_reduce(backward(True, *args), theirs_g, keep, send)

time: 118 us -> 116 us (0.983)
  waiting for transfers between devices: 28.4 us -> 26.2 us
  Pallas kernels: 22.6 us -> 24.5 us
    ppermute x15, waiting for transfers between devices: 19.6 us -> 16.7 us  [swap(): lax.ppermute(x, axis, [(i, i ^ k) for i in range(SIZES[AXES.index(axis)])])]
    pallas_call x7 -> x8, Pallas kernels: 13.2 us -> 15 us  [in_vmem(): pl.pallas_call(kernel, in_specs=[vm] * len(args), out_specs=[vm] * len(ou...]
    ppermute x12, waiting for transfers between devices: 4.1 us -> 5.81 us  [plane_swap(): return lax.ppermute(x, AXES, pairs)]
    ppermute x15, starting transfers between devices: 37.1 us -> 35.7 us  [swap(): lax.ppermute(x, axis, [(i, i ^ k) for i in range(SIZES[AXES.index(axis)])])]
  transfers between devices with their start and end apart: 34 -> 34, of which waited for: 16 -> 16; matrix products, arithmetic and copies ran while one was open for 1% -> 1% of each run, Pallas kernels for 12% -> 13%
where the time goes in v1:
time: 116 us
  starting transfers between devices  62.5 us (54%)
  waiting for transfers between devices  26.2 us (23%)
  Pallas kernels  24.5 us (21%)
  other arithmetic  1.69 us (1%)
    ppermute x15, starting transfers between devices, swap(): lax.ppermute(x, axis, [(i, i ^ k) for i in range(SIZES[AXES.index(axis)])])  35.7 us
    ppermute x15, waiting for transfers between devices, swap(): lax.ppermute(x, axis, [(i, i ^ k) for i in range(SIZES[AXES.index(axis)])])  16.7 us
    pallas_call x8, Pallas kernels, in_vmem(): pl.pallas_call(kernel, in_specs=[vm] * len(args), out_specs=[vm] * len(ou...  15 us
    ppermute x12, starting transfers between devices, plane_swap(): return lax.ppermute(x, AXES, pairs)  14.6 us
    ppermute x7, starting transfers between devices, shift(): return lax.ppermute(x, 'z', [(i, (i + by) % NZ) for i in range(NZ)])  12.2 us
    ppermute x12, waiting for transfers between devices, plane_swap(): return lax.ppermute(x, AXES, pairs)  5.81 us
    pallas_call x2, Pallas kernels, score(): pl.pallas_call(functools.partial(score_kernel, ks), in_specs=[vm] * (7 +...  4.79 us
    ppermute x7, waiting for transfers between devices, shift(): return lax.ppermute(x, 'z', [(i, (i + by) % NZ) for i in range(NZ)])  3.64 us
  transfers between devices with their start and end apart: 34, of which 16 were waited for; matrix products, arithmetic and copies ran while one was open for 1% of the time, Pallas kernels for 13%

profile of v1, /device:TPU:1, one launch (start us, length us, event | category | flops | bytes accessed | tf_op | source)
XLA Modules:
  0.0 116.1 jit_solution(9779398009757380720)
XLA Ops:
  0.7 2.0 %pack.1 = (bf16[272,256]{1,0:T(8,128)(2,1)}, bf16[528,256]{1,0:T(8,128)(2,1)}) custom-call(bf16[256,256]{1,0:T(8,128)(2,1)} %user_hbm.1, s32[1,256]{1,0:T(1,128)} %bitcast.54, bf16[512,256]{1,0:T(8,128)(2,1)} %feat_hbm.1, s32[1,512]{1,0:T(1,128)} %bitcast.52, s32[1,512]{1,0:T(1,128)} %bitcast.53), custom_call_target="tpu_custom_call" | custom-call | flops 10000000000 | bytes 1000000 | tf_op jit(solution)/shard_map/pack/pallas_call | solution.py:83
  2.6 2.5 %collective-permute-start.1 = (bf16[272,256]{1,0:T(8,128)(2,1)}, bf16[272,256]{1,0:T(8,128)(2,1)S(1)}, u32[]{:S(2)}, u32[]{:S(2)}) collective-permute-start(bf16[272,256]{1,0:T(8,128)(2,1)} %get-tuple-element.52.rest_0_), channel_id=1, source_target_pairs={{0,16},{16,32},{32,48},{48,64},{64,80},{80,96},{96,112},{112,0},{1... | collective-permute-start | bytes 417800 | tf_op jit(solution)/shard_map/ppermute | solution.py:371
  5.2 4.0 %collective-permute-start.2 = (bf16[272,256]{1,0:T(8,128)(2,1)}, bf16[272,256]{1,0:T(8,128)(2,1)S(1)}, u32[]{:S(2)}, u32[]{:S(2)}) collective-permute-start(bf16[272,256]{1,0:T(8,128)(2,1)} %get-tuple-element.52.rest_0_), channel_id=1, source_target_pairs={{0,112},{16,0},{32,16},{48,32},{64,48},{80,64},{96,80},{112,96},{1... | collective-permute-start | bytes 417800 | tf_op jit(solution)/shard_map/ppermute | solution.py:371
  12.7 2.7 %collective-permute-start.4 = (bf16[272,256]{1,0:T(8,128)(2,1)S(1)}, bf16[272,256]{1,0:T(8,128)(2,1)S(1)}, u32[]{:S(2)}, u32[]{:S(2)}) collective-permute-start(bf16[272,256]{1,0:T(8,128)(2,1)S(1)} %collective-permute-done.2.rest_2_), channel_id=1, source_target_pairs={{0,112},{16,0},{32,16},{48,32},{64,48},{80,64},{96,80},{112,96},{1... | collective-permute-start | bytes 417800 | tf_op jit(solution)/shard_map/ppermute | solution.py:371
  17.9 2.7 %collective-permute-start.6 = (bf16[272,256]{1,0:T(8,128)(2,1)S(1)}, bf16[272,256]{1,0:T(8,128)(2,1)S(1)}, u32[]{:S(2)}, u32[]{:S(2)}) collective-permute-start(bf16[272,256]{1,0:T(8,128)(2,1)S(1)} %collective-permute-done.4.rest_4_), channel_id=1, source_target_pairs={{0,112},{16,0},{32,16},{48,32},{64,48},{80,64},{96,80},{112,96},{1... | collective-permute-start | bytes 417800 | tf_op jit(solution)/shard_map/ppermute | solution.py:371
  20.5 2.9 %far.1 = (bf16[512,2048]{1,0:T(8,128)(2,1)S(1)}, bf16[512,256]{1,0:T(8,128)(2,1)S(1)}, f32[1024,128]{1,0:T(8,128)S(1)}, f32[1024,128]{1,0:T(8,128)S(1)}) custom-call(bf16[528,256]{1,0:T(8,128)(2,1)S(1)} %copy-done.3, bf16[528,256]{1,0:T(8,128)(2,1)S(1)} %collective-permute-done.far_ref, bf16[256,2048]{1,0:T(8,128)(2,1)S(1)} %get-tuple-element.46.w_in_ref, ...), custom_call_target="tpu_custom_call" | custom-call | flops 1073741824 | bytes 4000000 | tf_op jit(solution)/shard_map/far/pallas_call | solution.py:146
  23.8 3.7 %score.2 = (f32[8,256]{1,0:T(8,128)S(1)}, f32[8,256]{1,0:T(8,128)S(1)}, f32[1,256]{1,0:T(1,128)S(1)}, bf16[1024,1792]{1,0:T(8,128)(2,1)S(1)}) custom-call(bf16[512,256]{1,0:T(8,128)(2,1)S(1)} %get-tuple-element.44.near_emb, bf16[512,256]{1,0:T(8,128)(2,1)S(1)} %get-tuple-element.48.far_emb, f32[1024,128]{1,0:T(8,128)S(1)} %get-tuple-element.49.nid_ref, ...), custom_call_target="tpu_custom_call" | custom-call | flops 939524096 | bytes 5000000 | tf_op jit(solution)/shard_map/score/pallas_call | solution.py:206
  32.0 1.8 %collective-permute-start.8 = (f32[8,256]{1,0:T(8,128)S(1)}, f32[8,256]{1,0:T(8,128)S(1)}, u32[]{:S(2)}, u32[]{:S(2)}) collective-permute-start(f32[8,256]{1,0:T(8,128)S(1)} %get-tuple-element.60), channel_id=1, source_target_pairs={{0,16},{16,0},{32,48},{48,32},{64,80},{80,64},{96,112},{112,96},{1... | collective-permute-start | bytes 24584 | tf_op jit(solution)/shard_map/ppermute | solution.py:363
  33.8 2.0 %collective-permute-done.9 = f32[8,256]{1,0:T(8,128)S(1)} collective-permute-done((f32[8,256]{1,0:T(8,128)S(1)}, f32[8,256]{1,0:T(8,128)S(1)}, u32[]{:S(2)}, u32[]{:S(2)}) %collective-permute-start.9) | collective-permute-done | bytes 8224 | tf_op jit(solution)/shard_map/ppermute | solution.py:363
  35.8 1.8 %collective-permute-start.11 = (f32[8,256]{1,0:T(8,128)S(1)}, f32[8,256]{1,0:T(8,128)S(1)}, u32[]{:S(2)}, u32[]{:S(2)}) collective-permute-start(f32[8,256]{1,0:T(8,128)S(1)} %add_add_fusion), channel_id=1, source_target_pairs={{0,32},{16,48},{32,0},{48,16},{64,96},{80,112},{96,64},{112,80},{1... | collective-permute-start | bytes 24584 | tf_op jit(solution)/shard_map/ppermute | solution.py:363
  37.7 1.9 %collective-permute-done.11 = f32[8,256]{1,0:T(8,128)S(1)} collective-permute-done((f32[8,256]{1,0:T(8,128)S(1)}, f32[8,256]{1,0:T(8,128)S(1)}, u32[]{:S(2)}, u32[]{:S(2)}) %collective-permute-start.11) | collective-permute-done | bytes 8224 | tf_op jit(solution)/shard_map/ppermute | solution.py:363
  39.6 1.5 %items.1.g_ref = bf16[1280,256]{1,0:T(8,128)(2,1)S(1)} custom-call(f32[8,256]{1,0:T(8,128)S(1)} %add.63.tot_ref, f32[8,256]{1,0:T(8,128)S(1)} %get-tuple-element.61.tloc_ref, f32[1,256]{1,0:T(1,128)S(1)} %get-tuple-element.62.pexp_ref, bf16[1024,1792]{1,0:T(8,128)(2,1)S(1)} %get-tuple-element.63.kept_a, bf16[1024,256]{1,0:T(8,128)(2,1)S(1)} %get-tuple-element.64.kept_b, ...), custom_call_target="tpu_custom_call" | custom-call | flops 1073741824 | bytes 4000000 | tf_op jit(solution)/shard_map/items/pallas_call | solution.py:146
  41.1 3.1 %backward.3 = bf16[4,4,128,256]{3,2,1,0:T(8,128)(2,1)S(1)} custom-call(bf16[1280,256]{1,0:T(8,128)(2,1)S(1)} %items.1.g_ref, bf16[768,256]{1,0:T(8,128)(2,1)S(1)} %get-tuple-element.65.feat_ref, bf16[528,256]{1,0:T(8,128)(2,1)S(1)} %collective-permute-done.far_ref, bf16[2048,256]{1,0:T(8,128)(2,1)S(1)} %get-tuple-element.47.w_out_ref, ...), custom_call_target="tpu_custom_call" | custom-call | flops 2013265920 | bytes 4000000 | tf_op jit(solution)/shard_map/backward/pallas_call | solution.py:146
  44.3 5.8 %collective-permute-start.12 = (bf16[4,4,128,256]{3,2,1,0:T(8,128)(2,1)S(1)}, bf16[4,4,128,256]{3,2,1,0:T(8,128)(2,1)S(1)}, u32[]{:S(2)}, u32[]{:S(2)}) collective-permute-start(bf16[4,4,128,256]{3,2,1,0:T(8,128)(2,1)S(1)} %backward.3), channel_id=1, source_target_pairs={{0,1},{1,0},{2,3},{3,2},{4,5},{5,4},{6,7},{7,6},{8,9},{9,8},{10,11... | collective-permute-start | bytes 3145736 | tf_op jit(solution)/shard_map/ppermute | solution.py:363
  50.1 3.1 %backward.2 = bf16[4,4,128,256]{3,2,1,0:T(8,128)(2,1)S(1)} custom-call(bf16[1280,256]{1,0:T(8,128)(2,1)S(1)} %items.1.g_ref, bf16[768,256]{1,0:T(8,128)(2,1)S(1)} %get-tuple-element.65.feat_ref, bf16[528,256]{1,0:T(8,128)(2,1)S(1)} %collective-permute-done.far_ref, bf16[2048,256]{1,0:T(8,128)(2,1)S(1)} %get-tuple-element.47.w_out_ref, ...), custom_call_target="tpu_custom_call" | custom-call | flops 2013265920 | bytes 4000000 | tf_op jit(solution)/shard_map/backward/pallas_call | solution.py:146
  53.6 3.0 %collective-permute-start.13 = (bf16[4,128,256]{2,1,0:T(8,128)(2,1)S(1)}, bf16[4,128,256]{2,1,0:T(8,128)(2,1)S(1)}, u32[]{:S(2)}, u32[]{:S(2)}) collective-permute-start(bf16[4,128,256]{2,1,0:T(8,128)(2,1)S(1)} %get-tuple-element.83), channel_id=1, source_target_pairs={{0,8},{1,5},{2,10},{3,7},{4,12},{5,1},{6,14},{7,3},{128,136},{129,... | collective-permute-start | bytes 786440 | tf_op jit(solution)/shard_map/ppermute | solution.py:392
  58.4 1.6 %collective-permute-start.19 = (bf16[4,256,256]{2,1,0:T(8,128)(2,1)S(1)}, bf16[4,256,256]{2,1,0:T(8,128)(2,1)S(1)}, u32[]{:S(2)}, u32[]{:S(2)}) collective-permute-start(bf16[4,256,256]{2,1,0:T(8,128)(2,1)S(1)} %users.3), channel_id=1, source_target_pairs={{0,16},{16,0},{32,48},{48,32},{64,80},{80,64},{96,112},{112,96},{1... | collective-permute-start | bytes 1572872 | tf_op jit(solution)/shard_map/ppermute | solution.py:363
  61.0 3.0 %collective-permute-done.15 = bf16[4,128,256]{2,1,0:T(8,128)(2,1)S(1)} collective-permute-done((bf16[4,128,256]{2,1,0:T(8,128)(2,1)S(1)}, bf16[4,128,256]{2,1,0:T(8,128)(2,1)S(1)}, u32[]{:S(2)}, u32[]{:S(2)}) %collective-permute-start.15) | collective-permute-done | bytes 262176 | tf_op jit(solution)/shard_map/ppermute | solution.py:392
  64.1 2.8 %collective-permute-start.18 = (bf16[128,256]{1,0:T(8,128)(2,1)S(1)}, bf16[128,256]{1,0:T(8,128)(2,1)S(1)}, u32[]{:S(2)}, u32[]{:S(2)}) collective-permute-start(bf16[128,256]{1,0:T(8,128)(2,1)S(1)} %get-tuple-element.91), channel_id=1, source_target_pairs={{0,4},{1,9},{2,6},{3,11},{4,0},{5,13},{6,2},{7,15},{128,132},{129,... | collective-permute-start | bytes 196616 | tf_op jit(solution)/shard_map/ppermute | solution.py:392
  67.8 3.8 %collective-permute-done.19 = bf16[4,256,256]{2,1,0:T(8,128)(2,1)S(1)} collective-permute-done((bf16[4,256,256]{2,1,0:T(8,128)(2,1)S(1)}, bf16[4,256,256]{2,1,0:T(8,128)(2,1)S(1)}, u32[]{:S(2)}, u32[]{:S(2)}) %collective-permute-start.19) | collective-permute-done | bytes 524320 | tf_op jit(solution)/shard_map/ppermute | solution.py:363
  71.8 2.3 %collective-permute-start.22 = (bf16[128,256]{1,0:T(8,128)(2,1)S(1)}, bf16[128,256]{1,0:T(8,128)(2,1)S(1)}, u32[]{:S(2)}, u32[]{:S(2)}) collective-permute-start(bf16[128,256]{1,0:T(8,128)(2,1)S(1)} %fusion.7), channel_id=1, source_target_pairs={{0,96},{16,112},{32,64},{48,80},{64,32},{80,48},{96,0},{112,16},{1... | collective-permute-start | bytes 196616 | tf_op jit(solution)/shard_map/ppermute | solution.py:363
  74.1 1.6 %collective-permute-start.21 = (bf16[128,256]{1,0:T(8,128)(2,1)S(1)}, bf16[128,256]{1,0:T(8,128)(2,1)S(1)}, u32[]{:S(2)}, u32[]{:S(2)}) collective-permute-start(bf16[128,256]{1,0:T(8,128)(2,1)S(1)} %fusion.7), channel_id=1, source_target_pairs={{0,112},{16,96},{32,80},{48,64},{64,48},{80,32},{96,16},{112,0},{1... | collective-permute-start | bytes 196616 | tf_op jit(solution)/shard_map/ppermute | solution.py:363
  79.5 4.2 %collective-permute-start.23 = (bf16[128,256]{1,0:T(8,128)(2,1)S(1)}, bf16[128,256]{1,0:T(8,128)(2,1)S(1)}, u32[]{:S(2)}, u32[]{:S(2)}) collective-permute-start(bf16[128,256]{1,0:T(8,128)(2,1)S(1)} %add_convert_fusion.3), channel_id=1, source_target_pairs={{0,32},{16,48},{32,0},{48,16},{64,96},{80,112},{96,64},{112,80},{1... | collective-permute-start | bytes 196616 | tf_op jit(solution)/shard_map/ppermute | solution.py:363
  83.7 2.1 %collective-permute-done.23 = bf16[128,256]{1,0:T(8,128)(2,1)S(1)} collective-permute-done((bf16[128,256]{1,0:T(8,128)(2,1)S(1)}, bf16[128,256]{1,0:T(8,128)(2,1)S(1)}, u32[]{:S(2)}, u32[]{:S(2)}) %collective-permute-start.23) | collective-permute-done | bytes 65568 | tf_op jit(solution)/shard_map/ppermute | solution.py:363
  85.7 3.2 %collective-permute-start.26 = (bf16[128,256]{1,0:T(8,128)(2,1)S(1)}, bf16[128,256]{1,0:T(8,128)(2,1)S(1)}, u32[]{:S(2)}, u32[]{:S(2)}) collective-permute-start(bf16[128,256]{1,0:T(8,128)(2,1)S(1)} %add_convert_fusion.2), channel_id=1, source_target_pairs={{0,4},{1,9},{2,6},{3,11},{4,0},{5,13},{6,2},{7,15},{128,132},{129,... | collective-permute-start | bytes 196616 | tf_op jit(solution)/shard_map/ppermute | solution.py:392
  89.8 1.9 %collective-permute-start.30 = (bf16[256,256]{1,0:T(8,128)(2,1)S(1)}, bf16[256,256]{1,0:T(8,128)(2,1)S(1)}, u32[]{:S(2)}, u32[]{:S(2)}) collective-permute-start(bf16[256,256]{1,0:T(8,128)(2,1)S(1)} %get-tuple-element.86), channel_id=1, source_target_pairs={{0,64},{16,80},{32,96},{48,112},{64,0},{80,16},{96,32},{112,48},{1... | collective-permute-start | bytes 393224 | tf_op jit(solution)/shard_map/ppermute | solution.py:363
  91.8 3.2 %collective-permute-start.32 = (bf16[256,256]{1,0:T(8,128)(2,1)S(1)}, bf16[256,256]{1,0:T(8,128)(2,1)S(1)}, u32[]{:S(2)}, u32[]{:S(2)}) collective-permute-start(bf16[256,256]{1,0:T(8,128)(2,1)S(1)} %get-tuple-element.87), channel_id=1, source_target_pairs={{0,96},{16,112},{32,64},{48,80},{64,32},{80,48},{96,0},{112,16},{1... | collective-permute-start | bytes 393224 | tf_op jit(solution)/shard_map/ppermute | solution.py:363
  95.6 2.1 %collective-permute-start.29 = (bf16[4,128,256]{2,1,0:T(8,128)(2,1)S(1)}, bf16[4,128,256]{2,1,0:T(8,128)(2,1)S(1)}, u32[]{:S(2)}, u32[]{:S(2)}) collective-permute-start(bf16[4,128,256]{2,1,0:T(8,128)(2,1)S(1)} %get-tuple-element.90), channel_id=1, source_target_pairs={{0,8},{1,5},{2,10},{3,7},{4,12},{5,1},{6,14},{7,3},{128,136},{129,... | collective-permute-start | bytes 786440 | tf_op jit(solution)/shard_map/ppermute | solution.py:392
  98.8 1.4 %collective-permute-done.32 = bf16[256,256]{1,0:T(8,128)(2,1)S(1)} collective-permute-done((bf16[256,256]{1,0:T(8,128)(2,1)S(1)}, bf16[256,256]{1,0:T(8,128)(2,1)S(1)}, u32[]{:S(2)}, u32[]{:S(2)}) %collective-permute-start.32) | collective-permute-done | bytes 131104 | tf_op jit(solution)/shard_map/ppermute | solution.py:363
  100.3 2.4 %collective-permute-done.31 = bf16[256,256]{1,0:T(8,128)(2,1)S(1)} collective-permute-done((bf16[256,256]{1,0:T(8,128)(2,1)S(1)}, bf16[256,256]{1,0:T(8,128)(2,1)S(1)}, u32[]{:S(2)}, u32[]{:S(2)}) %collective-permute-start.31) | collective-permute-done | bytes 131104 | tf_op jit(solution)/shard_map/ppermute | solution.py:363
  102.8 2.8 %collective-permute-done.28 = bf16[4,128,256]{2,1,0:T(8,128)(2,1)S(1)} collective-permute-done((bf16[4,128,256]{2,1,0:T(8,128)(2,1)S(1)}, bf16[4,128,256]{2,1,0:T(8,128)(2,1)S(1)}, u32[]{:S(2)}, u32[]{:S(2)}) %collective-permute-start.28) | collective-permute-done | bytes 262176 | tf_op jit(solution)/shard_map/ppermute | solution.py:392
  105.7 6.5 %collective-permute-start.33 = (bf16[4,4,128,256]{3,2,1,0:T(8,128)(2,1)S(1)}, bf16[4,4,128,256]{3,2,1,0:T(8,128)(2,1)S(1)}, u32[]{:S(2)}, u32[]{:S(2)}) collective-permute-start(bf16[4,4,128,256]{3,2,1,0:T(8,128)(2,1)S(1)} %pad_maximum_fusion.x_ref), channel_id=1, source_target_pairs={{0,1},{1,0},{2,3},{3,2},{4,5},{5,4},{6,7},{7,6},{8,9},{9,8},{10,11... | collective-permute-start | bytes 3145736 | tf_op jit(solution)/shard_map/ppermute | solution.py:363
  (79 shorter events, 25.4 us)
Async XLA Ops:
  2.6 10.1 %collective-permute-start.1 = (bf16[272,256]{1,0:T(8,128)(2,1)}, bf16[272,256]{1,0:T(8,128)(2,1)S(1)}, u32[]{:S(2)}, u32[]{:S(2)}) collective-permute-start(bf16[272,256]{1,0:T(8,128)(2,1)} %get-tuple-element.52.rest_0_), channel_id=1, source_target_pairs={{0,16},{16,32},{32,48},{48,64},{64,80},{80,96},{96,112},{112,0},{1... | collective-permute-start | bytes 417800 | tf_op jit(solution)/shard_map/ppermute | solution.py:371
  5.2 7.6 %collective-permute-start.2 = (bf16[272,256]{1,0:T(8,128)(2,1)}, bf16[272,256]{1,0:T(8,128)(2,1)S(1)}, u32[]{:S(2)}, u32[]{:S(2)}) collective-permute-start(bf16[272,256]{1,0:T(8,128)(2,1)} %get-tuple-element.52.rest_0_), channel_id=1, source_target_pairs={{0,112},{16,0},{32,16},{48,32},{64,48},{80,64},{96,80},{112,96},{1... | collective-permute-start | bytes 417800 | tf_op jit(solution)/shard_map/ppermute | solution.py:371
  9.2 11.3 %collective-permute-start = (bf16[528,256]{1,0:T(8,128)(2,1)}, bf16[528,256]{1,0:T(8,128)(2,1)S(1)}, u32[]{:S(2)}, u32[]{:S(2)}) collective-permute-start(bf16[528,256]{1,0:T(8,128)(2,1)} %get-tuple-element.45.near_ref), channel_id=1, source_target_pairs={{0,128},{128,0},{1,129},{129,1},{2,130},{130,2},{3,131},{131,3},{4... | collective-permute-start | bytes 811016 | tf_op jit(solution)/shard_map/ppermute | solution.py:363
  12.7 5.1 %collective-permute-start.3 = (bf16[272,256]{1,0:T(8,128)(2,1)S(1)}, bf16[272,256]{1,0:T(8,128)(2,1)S(1)}, u32[]{:S(2)}, u32[]{:S(2)}) collective-permute-start(bf16[272,256]{1,0:T(8,128)(2,1)S(1)} %collective-permute-done.1.rest_1_), channel_id=1, source_target_pairs={{0,16},{16,32},{32,48},{48,64},{64,80},{80,96},{96,112},{112,0},{1... | collective-permute-start | bytes 417800 | tf_op jit(solution)/shard_map/ppermute | solution.py:371
  12.7 5.1 %collective-permute-start.4 = (bf16[272,256]{1,0:T(8,128)(2,1)S(1)}, bf16[272,256]{1,0:T(8,128)(2,1)S(1)}, u32[]{:S(2)}, u32[]{:S(2)}) collective-permute-start(bf16[272,256]{1,0:T(8,128)(2,1)S(1)} %collective-permute-done.2.rest_2_), channel_id=1, source_target_pairs={{0,112},{16,0},{32,16},{48,32},{64,48},{80,64},{96,80},{112,96},{1... | collective-permute-start | bytes 417800 | tf_op jit(solution)/shard_map/ppermute | solution.py:371
  17.9 5.6 %collective-permute-start.5 = (bf16[272,256]{1,0:T(8,128)(2,1)S(1)}, bf16[272,256]{1,0:T(8,128)(2,1)S(1)}, u32[]{:S(2)}, u32[]{:S(2)}) collective-permute-start(bf16[272,256]{1,0:T(8,128)(2,1)S(1)} %collective-permute-done.3.rest_3_), channel_id=1, source_target_pairs={{0,16},{16,32},{32,48},{48,64},{64,80},{80,96},{96,112},{112,0},{1... | collective-permute-start | bytes 417800 | tf_op jit(solution)/shard_map/ppermute | solution.py:371
  17.9 5.9 %collective-permute-start.6 = (bf16[272,256]{1,0:T(8,128)(2,1)S(1)}, bf16[272,256]{1,0:T(8,128)(2,1)S(1)}, u32[]{:S(2)}, u32[]{:S(2)}) collective-permute-start(bf16[272,256]{1,0:T(8,128)(2,1)S(1)} %collective-permute-done.4.rest_4_), channel_id=1, source_target_pairs={{0,112},{16,0},{32,16},{48,32},{64,48},{80,64},{96,80},{112,96},{1... | collective-permute-start | bytes 417800 | tf_op jit(solution)/shard_map/ppermute | solution.py:371
  23.5 5.4 %collective-permute-start.7 = (bf16[272,256]{1,0:T(8,128)(2,1)S(1)}, bf16[272,256]{1,0:T(8,128)(2,1)S(1)}, u32[]{:S(2)}, u32[]{:S(2)}) collective-permute-start(bf16[272,256]{1,0:T(8,128)(2,1)S(1)} %collective-permute-done.5.rest_5_), channel_id=1, source_target_pairs={{0,16},{16,32},{32,48},{48,64},{64,80},{80,96},{96,112},{112,0},{1... | collective-permute-start | bytes 417800 | tf_op jit(solution)/shard_map/ppermute | solution.py:371
  29.9 3.9 %collective-permute-start.10 = (f32[8,256]{1,0:T(8,128)S(1)}, f32[8,256]{1,0:T(8,128)S(1)}, u32[]{:S(2)}, u32[]{:S(2)}) collective-permute-start(f32[8,256]{1,0:T(8,128)S(1)} %get-tuple-element.60), channel_id=1, source_target_pairs={{0,112},{16,96},{32,80},{48,64},{64,48},{80,32},{96,16},{112,0},{1... | collective-permute-start | bytes 24584 | tf_op jit(solution)/shard_map/ppermute | solution.py:363
  31.2 4.6 %collective-permute-start.9 = (f32[8,256]{1,0:T(8,128)S(1)}, f32[8,256]{1,0:T(8,128)S(1)}, u32[]{:S(2)}, u32[]{:S(2)}) collective-permute-start(f32[8,256]{1,0:T(8,128)S(1)} %get-tuple-element.60), channel_id=1, source_target_pairs={{0,96},{16,112},{32,64},{48,80},{64,32},{80,48},{96,0},{112,16},{1... | collective-permute-start | bytes 24584 | tf_op jit(solution)/shard_map/ppermute | solution.py:363
  32.0 3.8 %collective-permute-start.8 = (f32[8,256]{1,0:T(8,128)S(1)}, f32[8,256]{1,0:T(8,128)S(1)}, u32[]{:S(2)}, u32[]{:S(2)}) collective-permute-start(f32[8,256]{1,0:T(8,128)S(1)} %get-tuple-element.60), channel_id=1, source_target_pairs={{0,16},{16,0},{32,48},{48,32},{64,80},{80,64},{96,112},{112,96},{1... | collective-permute-start | bytes 24584 | tf_op jit(solution)/shard_map/ppermute | solution.py:363
  44.3 8.9 %collective-permute-start.12 = (bf16[4,4,128,256]{3,2,1,0:T(8,128)(2,1)S(1)}, bf16[4,4,128,256]{3,2,1,0:T(8,128)(2,1)S(1)}, u32[]{:S(2)}, u32[]{:S(2)}) collective-permute-start(bf16[4,4,128,256]{3,2,1,0:T(8,128)(2,1)S(1)} %backward.3), channel_id=1, source_target_pairs={{0,1},{1,0},{2,3},{3,2},{4,5},{5,4},{6,7},{7,6},{8,9},{9,8},{10,11... | collective-permute-start | bytes 3145736 | tf_op jit(solution)/shard_map/ppermute | solution.py:363
  53.6 7.3 %collective-permute-start.13 = (bf16[4,128,256]{2,1,0:T(8,128)(2,1)S(1)}, bf16[4,128,256]{2,1,0:T(8,128)(2,1)S(1)}, u32[]{:S(2)}, u32[]{:S(2)}) collective-permute-start(bf16[4,128,256]{2,1,0:T(8,128)(2,1)S(1)} %get-tuple-element.83), channel_id=1, source_target_pairs={{0,8},{1,5},{2,10},{3,7},{4,12},{5,1},{6,14},{7,3},{128,136},{129,... | collective-permute-start | bytes 786440 | tf_op jit(solution)/shard_map/ppermute | solution.py:392
  56.7 7.3 %collective-permute-start.15 = (bf16[4,128,256]{2,1,0:T(8,128)(2,1)S(1)}, bf16[4,128,256]{2,1,0:T(8,128)(2,1)S(1)}, u32[]{:S(2)}, u32[]{:S(2)}) collective-permute-start(bf16[4,128,256]{2,1,0:T(8,128)(2,1)S(1)} %get-tuple-element.84), channel_id=1, source_target_pairs={{0,128},{1,3},{2,130},{3,1},{4,132},{5,7},{6,134},{7,5},{128,0},{1... | collective-permute-start | bytes 786440 | tf_op jit(solution)/shard_map/ppermute | solution.py:392
  57.1 6.9 %collective-permute-start.14 = (bf16[4,128,256]{2,1,0:T(8,128)(2,1)S(1)}, bf16[4,128,256]{2,1,0:T(8,128)(2,1)S(1)}, u32[]{:S(2)}, u32[]{:S(2)}) collective-permute-start(bf16[4,128,256]{2,1,0:T(8,128)(2,1)S(1)} %get-tuple-element.85), channel_id=1, source_target_pairs={{0,136},{1,7},{2,138},{3,5},{4,140},{5,3},{6,142},{7,1},{128,8},{1... | collective-permute-start | bytes 786440 | tf_op jit(solution)/shard_map/ppermute | solution.py:392
  58.4 13.2 %collective-permute-start.19 = (bf16[4,256,256]{2,1,0:T(8,128)(2,1)S(1)}, bf16[4,256,256]{2,1,0:T(8,128)(2,1)S(1)}, u32[]{:S(2)}, u32[]{:S(2)}) collective-permute-start(bf16[4,256,256]{2,1,0:T(8,128)(2,1)S(1)} %users.3), channel_id=1, source_target_pairs={{0,16},{16,0},{32,48},{48,32},{64,80},{80,64},{96,112},{112,96},{1... | collective-permute-start | bytes 1572872 | tf_op jit(solution)/shard_map/ppermute | solution.py:363
  64.1 7.6 %collective-permute-start.18 = (bf16[128,256]{1,0:T(8,128)(2,1)S(1)}, bf16[128,256]{1,0:T(8,128)(2,1)S(1)}, u32[]{:S(2)}, u32[]{:S(2)}) collective-permute-start(bf16[128,256]{1,0:T(8,128)(2,1)S(1)} %get-tuple-element.91), channel_id=1, source_target_pairs={{0,4},{1,9},{2,6},{3,11},{4,0},{5,13},{6,2},{7,15},{128,132},{129,... | collective-permute-start | bytes 196616 | tf_op jit(solution)/shard_map/ppermute | solution.py:392
  66.9 4.8 %collective-permute-start.17 = (bf16[128,256]{1,0:T(8,128)(2,1)S(1)}, bf16[128,256]{1,0:T(8,128)(2,1)S(1)}, u32[]{:S(2)}, u32[]{:S(2)}) collective-permute-start(bf16[128,256]{1,0:T(8,128)(2,1)S(1)} %get-tuple-element.92), channel_id=1, source_target_pairs={{0,6},{1,137},{2,4},{3,139},{4,2},{5,141},{6,0},{7,143},{128,134},... | collective-permute-start | bytes 196616 | tf_op jit(solution)/shard_map/ppermute | solution.py:392
  67.8 4.0 %collective-permute-start.16 = (bf16[128,256]{1,0:T(8,128)(2,1)S(1)}, bf16[128,256]{1,0:T(8,128)(2,1)S(1)}, u32[]{:S(2)}, u32[]{:S(2)}) collective-permute-start(bf16[128,256]{1,0:T(8,128)(2,1)S(1)} %get-tuple-element.93), channel_id=1, source_target_pairs={{0,2},{1,129},{2,0},{3,131},{4,6},{5,133},{6,4},{7,135},{128,130},... | collective-permute-start | bytes 196616 | tf_op jit(solution)/shard_map/ppermute | solution.py:392
  71.8 5.4 %collective-permute-start.22 = (bf16[128,256]{1,0:T(8,128)(2,1)S(1)}, bf16[128,256]{1,0:T(8,128)(2,1)S(1)}, u32[]{:S(2)}, u32[]{:S(2)}) collective-permute-start(bf16[128,256]{1,0:T(8,128)(2,1)S(1)} %fusion.7), channel_id=1, source_target_pairs={{0,96},{16,112},{32,64},{48,80},{64,32},{80,48},{96,0},{112,16},{1... | collective-permute-start | bytes 196616 | tf_op jit(solution)/shard_map/ppermute | solution.py:363
  74.1 4.4 %collective-permute-start.21 = (bf16[128,256]{1,0:T(8,128)(2,1)S(1)}, bf16[128,256]{1,0:T(8,128)(2,1)S(1)}, u32[]{:S(2)}, u32[]{:S(2)}) collective-permute-start(bf16[128,256]{1,0:T(8,128)(2,1)S(1)} %fusion.7), channel_id=1, source_target_pairs={{0,112},{16,96},{32,80},{48,64},{64,48},{80,32},{96,16},{112,0},{1... | collective-permute-start | bytes 196616 | tf_op jit(solution)/shard_map/ppermute | solution.py:363
  79.5 6.3 %collective-permute-start.23 = (bf16[128,256]{1,0:T(8,128)(2,1)S(1)}, bf16[128,256]{1,0:T(8,128)(2,1)S(1)}, u32[]{:S(2)}, u32[]{:S(2)}) collective-permute-start(bf16[128,256]{1,0:T(8,128)(2,1)S(1)} %add_convert_fusion.3), channel_id=1, source_target_pairs={{0,32},{16,48},{32,0},{48,16},{64,96},{80,112},{96,64},{112,80},{1... | collective-permute-start | bytes 196616 | tf_op jit(solution)/shard_map/ppermute | solution.py:363
  85.7 9.2 %collective-permute-start.26 = (bf16[128,256]{1,0:T(8,128)(2,1)S(1)}, bf16[128,256]{1,0:T(8,128)(2,1)S(1)}, u32[]{:S(2)}, u32[]{:S(2)}) collective-permute-start(bf16[128,256]{1,0:T(8,128)(2,1)S(1)} %add_convert_fusion.2), channel_id=1, source_target_pairs={{0,4},{1,9},{2,6},{3,11},{4,0},{5,13},{6,2},{7,15},{128,132},{129,... | collective-permute-start | bytes 196616 | tf_op jit(solution)/shard_map/ppermute | solution.py:392
  88.9 6.7 %collective-permute-start.25 = (bf16[128,256]{1,0:T(8,128)(2,1)S(1)}, bf16[128,256]{1,0:T(8,128)(2,1)S(1)}, u32[]{:S(2)}, u32[]{:S(2)}) collective-permute-start(bf16[128,256]{1,0:T(8,128)(2,1)S(1)} %add_convert_fusion.2), channel_id=1, source_target_pairs={{0,6},{1,137},{2,4},{3,139},{4,2},{5,141},{6,0},{7,143},{128,134},... | collective-permute-start | bytes 196616 | tf_op jit(solution)/shard_map/ppermute | solution.py:392
  89.8 5.8 %collective-permute-start.24 = (bf16[128,256]{1,0:T(8,128)(2,1)S(1)}, bf16[128,256]{1,0:T(8,128)(2,1)S(1)}, u32[]{:S(2)}, u32[]{:S(2)}) collective-permute-start(bf16[128,256]{1,0:T(8,128)(2,1)S(1)} %add_convert_fusion.2), channel_id=1, source_target_pairs={{0,2},{1,129},{2,0},{3,131},{4,6},{5,133},{6,4},{7,135},{128,130},... | collective-permute-start | bytes 196616 | tf_op jit(solution)/shard_map/ppermute | solution.py:392
  89.8 8.7 %collective-permute-start.30 = (bf16[256,256]{1,0:T(8,128)(2,1)S(1)}, bf16[256,256]{1,0:T(8,128)(2,1)S(1)}, u32[]{:S(2)}, u32[]{:S(2)}) collective-permute-start(bf16[256,256]{1,0:T(8,128)(2,1)S(1)} %get-tuple-element.86), channel_id=1, source_target_pairs={{0,64},{16,80},{32,96},{48,112},{64,0},{80,16},{96,32},{112,48},{1... | collective-permute-start | bytes 393224 | tf_op jit(solution)/shard_map/ppermute | solution.py:363
  91.8 8.5 %collective-permute-start.32 = (bf16[256,256]{1,0:T(8,128)(2,1)S(1)}, bf16[256,256]{1,0:T(8,128)(2,1)S(1)}, u32[]{:S(2)}, u32[]{:S(2)}) collective-permute-start(bf16[256,256]{1,0:T(8,128)(2,1)S(1)} %get-tuple-element.87), channel_id=1, source_target_pairs={{0,96},{16,112},{32,64},{48,80},{64,32},{80,48},{96,0},{112,16},{1... | collective-permute-start | bytes 393224 | tf_op jit(solution)/shard_map/ppermute | solution.py:363
  95.0 7.7 %collective-permute-start.31 = (bf16[256,256]{1,0:T(8,128)(2,1)S(1)}, bf16[256,256]{1,0:T(8,128)(2,1)S(1)}, u32[]{:S(2)}, u32[]{:S(2)}) collective-permute-start(bf16[256,256]{1,0:T(8,128)(2,1)S(1)} %get-tuple-element.88), channel_id=1, source_target_pairs={{0,32},{16,48},{32,0},{48,16},{64,96},{80,112},{96,64},{112,80},{1... | collective-permute-start | bytes 393224 | tf_op jit(solution)/shard_map/ppermute | solution.py:363
  95.6 7.1 %collective-permute-start.29 = (bf16[4,128,256]{2,1,0:T(8,128)(2,1)S(1)}, bf16[4,128,256]{2,1,0:T(8,128)(2,1)S(1)}, u32[]{:S(2)}, u32[]{:S(2)}) collective-permute-start(bf16[4,128,256]{2,1,0:T(8,128)(2,1)S(1)} %get-tuple-element.90), channel_id=1, source_target_pairs={{0,8},{1,5},{2,10},{3,7},{4,12},{5,1},{6,14},{7,3},{128,136},{129,... | collective-permute-start | bytes 786440 | tf_op jit(solution)/shard_map/ppermute | solution.py:392
  97.7 7.8 %collective-permute-start.28 = (bf16[4,128,256]{2,1,0:T(8,128)(2,1)S(1)}, bf16[4,128,256]{2,1,0:T(8,128)(2,1)S(1)}, u32[]{:S(2)}, u32[]{:S(2)}) collective-permute-start(bf16[4,128,256]{2,1,0:T(8,128)(2,1)S(1)} %get-tuple-element.90), channel_id=1, source_target_pairs={{0,136},{1,7},{2,138},{3,5},{4,140},{5,3},{6,142},{7,1},{128,8},{1... | collective-permute-start | bytes 786440 | tf_op jit(solution)/shard_map/ppermute | solution.py:392
  98.6 7.0 %collective-permute-start.27 = (bf16[4,128,256]{2,1,0:T(8,128)(2,1)S(1)}, bf16[4,128,256]{2,1,0:T(8,128)(2,1)S(1)}, u32[]{:S(2)}, u32[]{:S(2)}) collective-permute-start(bf16[4,128,256]{2,1,0:T(8,128)(2,1)S(1)} %get-tuple-element.90), channel_id=1, source_target_pairs={{0,128},{1,3},{2,130},{3,1},{4,132},{5,7},{6,134},{7,5},{128,0},{1... | collective-permute-start | bytes 786440 | tf_op jit(solution)/shard_map/ppermute | solution.py:392
  105.7 8.8 %collective-permute-start.33 = (bf16[4,4,128,256]{3,2,1,0:T(8,128)(2,1)S(1)}, bf16[4,4,128,256]{3,2,1,0:T(8,128)(2,1)S(1)}, u32[]{:S(2)}, u32[]{:S(2)}) collective-permute-start(bf16[4,4,128,256]{3,2,1,0:T(8,128)(2,1)S(1)} %pad_maximum_fusion.x_ref), channel_id=1, source_target_pairs={{0,1},{1,0},{2,3},{3,2},{4,5},{5,4},{6,7},{7,6},{8,9},{9,8},{10,11... | collective-permute-start | bytes 3145736 | tf_op jit(solution)/shard_map/ppermute | solution.py:363
  (9 other events, 72.2 us)
